TPU v7x, 256 devices: a whole 4x4x8 slice. The times are simulated.
256 devices in a mesh: dp: 16 (over z, core), mp: 16 (over x, y).
Axes of the slice: x: 4, y: 4, z: 8, core: 2. Of those that a mesh axis runs over, the one named last changes fastest.
Arguments:
- queries: bfloat16 [8192, 4096], P('dp', 'mp'), may hold values from -60 to 60
- grad_attn: bfloat16 [8192, 4096], P('dp', 'mp'), may hold values from -6 to 6
- encoded: bfloat16 [8192, 4096], P('dp', 'mp'), may hold values from -6 to 6
- key_weight: bfloat16 [4096, 4096], P(None, 'mp'), may hold values from -0.09375 to 0.09375
- value_weight: bfloat16 [4096, 4096], P(None, 'mp'), may hold values from -0.09375 to 0.09375
- nbr_ids: int32 [128, 2], P('dp'), may hold values from 0 to 63, as said below
Outputs:
- query_grad: bfloat16 [8192, 4096], P('dp', 'mp')
- encoded_grad: bfloat16 [8192, 4096], P('dp', 'mp')
- key_weight_grad: float32 [4096, 4096], P('dp', 'mp')
- value_weight_grad: float32 [4096, 4096], P('dp', 'mp')
Inputs may be any that keep to these rules, and one draw needn't show every extreme that they name: `nbr_ids`: of the 16 slots of one index of dp, at most 2 name blocks of one owner (owner = id // 4); in every draw one owner gets exactly 2 from every index. The 2 neighbours of a span differ.
All inputs are finite; a program needn't handle non-finite values.
Results may differ from a plain program's by a relative error of at most 0.015.
The roundings to bfloat16 on the way count: a program that leaves them out, or rounds other values in their place, can miss the bound.
Values may be sent and summed in bfloat16 or wider, within the bound.
A program may use at most 128 MiB of HBM per device.

v0:
```python
import math

import jax
import jax.numpy as jnp
from jax import lax
from jax.sharding import PartitionSpec as P

HD = 128
SPAN = 64
NL = 128
K = 2
NB_DEV = 4


def slot_ranks(owners):
    slot_count = owners.shape[-1]
    position = jnp.arange(slot_count, dtype=jnp.int32)
    alike = (owners[..., :, None] == owners[..., None, :]) & (position[None, :] < position[:, None])
    return jnp.sum(alike.astype(jnp.int32), axis=-1)


def body(queries, grad_attn, encoded, key_weight, value_weight, nbr_ids):
    head_cols = key_weight.shape[1]
    model_width = key_weight.shape[0]
    heads_here = head_cols // HD
    enc_rows = encoded.shape[0]
    dp_count = lax.axis_size("dp")
    owner_here = lax.axis_index("dp")
    span_count = nbr_ids.shape[0]
    slot_count = span_count * K
    capacity = max(2, 2 * slot_count // dp_count)
    scale = 1.0 / math.sqrt(HD)
    both_weights = jnp.concatenate([key_weight, value_weight], axis=1)
    whole_enc = lax.all_gather(encoded, "mp", axis=1, tiled=True)
    projected = jnp.dot(whole_enc, both_weights, preferred_element_type=jnp.float32)
    kv_blocks = projected.astype(jnp.bfloat16).reshape(NB_DEV, NL, 2 * head_cols)
    every_ids = lax.all_gather(nbr_ids, "dp", axis=0, tiled=True).reshape(dp_count, slot_count)
    all_owners = every_ids // NB_DEV
    local_block = every_ids % NB_DEV
    all_ranks = slot_ranks(all_owners)
    slot_axis = jnp.arange(capacity, dtype=jnp.int32)
    matched = (all_owners == owner_here)[:, :, None] & (
        all_ranks[:, :, None] == slot_axis[None, None, :]
    )
    picked = jnp.sum(jnp.where(matched, local_block[:, :, None], 0), axis=1)
    filled = jnp.any(matched, axis=1)
    outgoing = jnp.where(filled[:, :, None, None], kv_blocks[picked], jnp.zeros((), jnp.bfloat16))
    received = lax.all_to_all(outgoing, "dp", split_axis=0, concat_axis=0, tiled=True)
    own_ids = nbr_ids.reshape(slot_count)
    own_owners = own_ids // NB_DEV
    flat_slot = own_owners * capacity + slot_ranks(own_owners)
    slot_kv = received.reshape(dp_count * capacity, NL, 2 * head_cols)[flat_slot]
    slot_kv = slot_kv.reshape(span_count, K * NL, 2, heads_here, HD)
    key_blocks = slot_kv[:, :, 0]
    value_blocks = slot_kv[:, :, 1]
    query_blocks = queries.reshape(span_count, SPAN, heads_here, HD)
    grad_blocks = grad_attn.reshape(span_count, SPAN, heads_here, HD)
    scores = (
        jnp.einsum("cqhd,ckhd->chqk", query_blocks, key_blocks, preferred_element_type=jnp.float32)
        * scale
    )
    attn_prob = jax.nn.softmax(scores, axis=-1)
    prob_rounded = attn_prob.astype(jnp.bfloat16)
    prob_grad = jnp.einsum(
        "cqhd,ckhd->chqk", grad_blocks, value_blocks, preferred_element_type=jnp.float32
    )
    delta = jnp.sum(attn_prob * prob_grad, axis=-1, keepdims=True)
    score_grad = (attn_prob * (prob_grad - delta) * scale).astype(jnp.bfloat16)
    query_grad = jnp.einsum(
        "chqk,ckhd->cqhd", score_grad, key_blocks, preferred_element_type=jnp.float32
    )
    slot_key = jnp.einsum(
        "chqk,cqhd->ckhd", score_grad, query_blocks, preferred_element_type=jnp.float32
    ).astype(jnp.bfloat16)
    slot_value = jnp.einsum(
        "chqk,cqhd->ckhd", prob_rounded, grad_blocks, preferred_element_type=jnp.float32
    ).astype(jnp.bfloat16)
    slot_grad = jnp.stack([slot_key, slot_value], axis=2).reshape(slot_count, NL, 2 * head_cols)
    return_buf = (
        jnp.zeros((dp_count * capacity, NL, 2 * head_cols), jnp.bfloat16)
        .at[flat_slot]
        .set(slot_grad)
    )
    returned = lax.all_to_all(
        return_buf.reshape(dp_count, capacity, NL, 2 * head_cols),
        "dp",
        split_axis=0,
        concat_axis=0,
        tiled=True,
    )
    block_axis = jnp.arange(NB_DEV, dtype=jnp.int32)
    selector = (filled[:, :, None] & (picked[:, :, None] == block_axis[None, None, :])).astype(
        jnp.bfloat16
    )
    selector = selector.reshape(dp_count * capacity, NB_DEV)
    block_grad = jnp.einsum(
        "nb,nlc->blc",
        selector,
        returned.reshape(dp_count * capacity, NL, 2 * head_cols),
        preferred_element_type=jnp.float32,
    )
    block_grad = block_grad.astype(jnp.bfloat16).reshape(enc_rows, 2 * head_cols)
    contract_cols = (((1,), (1,)), ((), ()))
    width_terms = lax.dot_general(
        block_grad, both_weights, contract_cols, preferred_element_type=jnp.float32
    )
    encoded_grad = lax.psum_scatter(width_terms, "mp", scatter_dimension=1, tiled=True).astype(
        jnp.bfloat16
    )
    contract_rows = (((0,), (0,)), ((), ()))
    weight_grad = lax.psum_scatter(
        lax.dot_general(whole_enc, block_grad, contract_rows, preferred_element_type=jnp.float32),
        "dp",
        scatter_dimension=0,
        tiled=True,
    )
    weight_grad = weight_grad.reshape(model_width // dp_count, 2, heads_here, HD)
    key_weight_grad = weight_grad[:, 0].reshape(model_width // dp_count, head_cols)
    value_weight_grad = weight_grad[:, 1].reshape(model_width // dp_count, head_cols)
    query_grad = query_grad.astype(jnp.bfloat16).reshape(span_count * SPAN, head_cols)
    return (query_grad, encoded_grad, key_weight_grad, value_weight_grad)


def solution(mesh):
    return jax.shard_map(
        body,
        mesh=mesh,
        in_specs=(
            P("dp", "mp"),
            P("dp", "mp"),
            P("dp", "mp"),
            P(None, "mp"),
            P(None, "mp"),
            P("dp", None),
        ),
        out_specs=(P("dp", "mp"), P("dp", "mp"), P("dp", "mp"), P("dp", "mp")),
        check_vma=False,
    )
```

profile of v0, /device:TPU:2, one launch (start us, length us, event | category | flops | bytes accessed | tf_op | source)
XLA Modules:
  0.0 510.0 jit_solution(6797718014809337853)
XLA Ops:
  7.9 20.2 %all-gather = s32[16,8,2]{1,2,0:T(2,128)S(1)} all-gather(s32[1,8,2]{1,2,0:T(2,128)} %bitcast.79), channel_id=1, replica_groups=mesh['dp'=16,'mp'=16] {'dp'}, dimensions={0}, use_global_device_ids=true | all-gather | bytes 1088 | tf_op jit(solution)/shard_map/all_gather | solution.py:37
  29.5 3.1 constant_dynamic-update-slice_fusion.1
  32.6 1.5 constant_dynamic-update-slice_fusion
  34.1 41.6 %all-gather.3.cloned.1.call-done = bf16[512,4096]{1,0:T(8,128)(2,1)} async-done(((bf16[512,256]{1,0:T(8,128)(2,1)}), bf16[512,4096]{1,0:T(8,128)(2,1)}) %all-gather.3.cloned.1.call-update) | async-done | bytes 4194320 | tf_op jit(solution)/shard_map/all_gather | solution.py:34
  75.7 5.8 %convolution_convert_fusion.2 = bf16[512,512]{0,1:T(8,128)(2,1)S(1)} fusion(bf16[512,4096]{1,0:T(8,128)(2,1)} %all-gather.3.cloned.1.call-done, bf16[4096,512]{1,0:T(8,128)(2,1)} %constant_dynamic-update-slice_fusion), kind=kOutput, calls=%fused_computation.24 | convolution fusion | flops 2147745792 | bytes 8912896 | tf_op jit(solution)/shard_map/dot_general | solution.py:35
  81.5 2.8 gather_fusion
  84.2 4.5 broadcast_select_fusion
  88.8 7.3 %all-to-all-start = ((bf16[16,2,128,512]{3,2,1,0:T(8,128)(2,1)}), bf16[16,2,128,512]{3,2,1,0:T(8,128)(2,1)}, u32[]{:S(2)}, u32[]{:S(2)}) async-start(bf16[16,2,128,512]{3,2,1,0:T(8,128)(2,1)} %broadcast_select_fusion), calls=%async_computation | async-start | bytes 8388608 | tf_op jit(solution)/shard_map/all_to_all | solution.py:48
  97.4 92.9 %all-to-all-done = bf16[16,2,128,512]{3,2,1,0:T(8,128)(2,1)} async-done(((bf16[16,2,128,512]{3,2,1,0:T(8,128)(2,1)}), bf16[16,2,128,512]{3,2,1,0:T(8,128)(2,1)}, u32[]{:S(2)}, u32[]{:S(2)}) %all-to-all-start) | async-done | bytes 4194336 | tf_op jit(solution)/shard_map/all_to_all | solution.py:48
  190.4 4.3 gather_fusion.1
  194.6 2.5 reshape.336
  197.2 1.5 fusion.46
  199.2 1.2 fusion.48
  200.4 1.5 convolution_bitcast_fusion.1
  201.9 3.2 fusion.6
  205.1 8.4 %fusion.5 = bf16[8,256,1,2,128]{4,1,3,0,2:T(8,128)(2,1)S(1)} fusion(f32[8,2,64,256]{3,2,1,0:T(8,128)} %convolution_bitcast_fusion.1, bf16[8,64,2,128]{3,2,1,0:T(2,128)(2,1)S(1)} %reshape.299, f32[8,2,64,256]{3,2,1,0:T(8,128)} %get-tuple-element.11, f32[8,2,64]{2,1,0:T(2,128)S(1)} %get-tuple-element.10), kind=kOutput, calls=%fused_computation.13 | convolution fusion | flops 69469440 | bytes 3411968 | tf_op jit(solution)/shard_map/chqk,cqhd->ckhd/dot_general | solution.py:72
  213.8 3.5 copy.116
  217.2 2.7 reshape.337
  220.0 2.4 broadcast_in_dim.30
  222.4 5.2 %scatter_fusion = bf16[32,128,512]{2,1,0:T(8,128)(2,1)} fusion(bf16[32,128,512]{2,1,0:T(8,128)(2,1)} %broadcast_in_dim.30, s32[16]{0:T(128)S(1)} %fusion.41, bf16[16,128,512]{2,1,0:T(8,128)(2,1)S(1)} %reshape.337), kind=kCustom, calls=%fused_computation.2 | custom fusion | bytes 6291520 | tf_op jit(solution)/shard_map/scatter | solution.py:82
  227.6 6.5 %copy.107 = bf16[16,2,128,512]{3,1,2,0:T(2,128)(2,1)S(1)} copy(bf16[16,2,128,512]{3,2,1,0:T(8,128)(2,1)} %bitcast.68) | data formatting | bytes 8388608 | tf_op jit(solution)/shard_map/reshape | solution.py:85
  234.2 99.2 %all_to_all.10 = bf16[16,2,128,512]{3,1,2,0:T(2,128)(2,1)S(1)} all-to-all(bf16[16,2,128,512]{3,1,2,0:T(2,128)(2,1)S(1)} %copy.107), channel_id=1, replica_groups=mesh['dp'=16,'mp'=16] {'dp'}, dimensions={0} | all-to-all | bytes 8388608 | tf_op jit(solution)/shard_map/all_to_all | solution.py:84
  333.4 2.5 fusion.15
  336.0 5.7 %convolution_bitcast_fusion = f32[4096,512]{0,1:T(8,128)} fusion(bf16[512,512]{1,0:T(8,128)(2,1)S(1)} %bitcast.70, bf16[512,4096]{1,0:T(8,128)(2,1)S(1)} %copy-done), kind=kOutput, calls=%fused_computation.5 | convolution fusion | flops 2147483648 | bytes 13107200 | tf_op jit(solution)/shard_map/dot_general | solution.py:112
  342.0 7.8 %fusion.49 = f32[512,4096]{1,0:T(8,128)} fusion(bf16[512,512]{1,0:T(8,128)(2,1)S(1)} %bitcast.71, bf16[4096,512]{1,0:T(8,128)(2,1)} %constant_dynamic-update-slice_fusion), kind=kOutput, calls=%fused_computation.85 | convolution fusion | flops 2147483648 | bytes 13107200 | tf_op jit(solution)/shard_map/dot_general | solution.py:104
  349.8 7.7 %fusion.19 = bf16[8,64,2,128]{3,1,2,0:T(8,128)(2,1)S(1)} fusion(f32[8,2,64,256]{3,2,1,0:T(8,128)} %convolution_bitcast_fusion.1, bf16[8,256,1,2,128]{4,3,2,1,0:T(2,128)(2,1)S(1)} %get-tuple-element.6, f32[8,2,64,256]{3,2,1,0:T(8,128)} %get-tuple-element.11, f32[8,2,64]{2,1,0:T(2,128)S(1)} %get-tuple-element.10), kind=kOutput, calls=%fused_computation.27 | convolution fusion | flops 69076224 | bytes 3411968 | tf_op jit(solution)/shard_map/chqk,ckhd->cqhd/dot_general | solution.py:69
  358.5 50.9 %reduce-scatter.5.cloned.1.call-done = f32[256,512]{0,1:T(8,128)} async-done(((f32[4096,512]{0,1:T(8,128)}), f32[256,512]{0,1:T(8,128)}) %reduce-scatter.5.cloned.1.call-update) | async-done | bytes 524304 | tf_op jit(solution)/shard_map/reduce_scatter | solution.py:111
  409.4 1.1 fusion.47
  410.4 0.8 copy.118
  411.3 0.8 copy.117
  412.1 89.6 %reduce-scatter.3.cloned.1.call-done = f32[512,256]{1,0:T(8,128)} async-done(((f32[512,4096]{1,0:T(8,128)}), f32[512,256]{1,0:T(8,128)}) %reduce-scatter.3.cloned.1.call-update) | async-done | bytes 524304 | tf_op jit(solution)/shard_map/reduce_scatter | solution.py:107
  501.7 1.8 convert_element_type.56
  (51 shorter events, 5.5 us)
Async XLA Ops:
  7.2 25.4 %copy-start.1 = (bf16[4096,256]{1,0:T(8,128)(2,1)S(1)}, bf16[4096,256]{1,0:T(8,128)(2,1)}, u32[]{:S(2)}) copy-start(bf16[4096,256]{1,0:T(8,128)(2,1)} %param.10) | copy-start | bytes 6291460
  7.2 68.5 %all-gather.3.cloned.1.call-start = ((), (), s32[]{:S(2)}) async-start(), calls=%async_computation.4 | async-start | bytes 4456448 | tf_op jit(solution)/shard_map/all_gather | solution.py:34
  88.8 7.4 %copy-start.7 = (s32[8,2]{0,1:T(2,128)S(1)}, s32[8,2]{0,1:T(2,128)}, u32[]{:S(2)}) copy-start(s32[8,2]{0,1:T(2,128)} %param.11) | copy-start | bytes 196
  88.8 7.6 %copy-start.5 = (bf16[512,256]{1,0:T(8,128)(2,1)S(1)}, bf16[512,256]{1,0:T(8,128)(2,1)}, u32[]{:S(2)}) copy-start(bf16[512,256]{1,0:T(8,128)(2,1)} %param.6) | copy-start | bytes 786436
  88.8 7.7 %copy-start.6 = (bf16[512,256]{1,0:T(8,128)(2,1)S(1)}, bf16[512,256]{1,0:T(8,128)(2,1)}, u32[]{:S(2)}) copy-start(bf16[512,256]{1,0:T(8,128)(2,1)} %param.7) | copy-start | bytes 786436
  88.8 101.6 %all-to-all-start = ((bf16[16,2,128,512]{3,2,1,0:T(8,128)(2,1)}), bf16[16,2,128,512]{3,2,1,0:T(8,128)(2,1)}, u32[]{:S(2)}, u32[]{:S(2)}) async-start(bf16[16,2,128,512]{3,2,1,0:T(8,128)(2,1)} %broadcast_select_fusion), calls=%async_computation | async-start | bytes 8388608 | tf_op jit(solution)/shard_map/all_to_all | solution.py:48
  96.1 313.3 %reduce-scatter.5.cloned.1.call-start = ((), (), s32[]{:S(2)}) async-start(), calls=%async_computation.6 | async-start | bytes 8912896 | tf_op jit(solution)/shard_map/reduce_scatter | solution.py:111
  197.2 3.2 copy-start.2
  198.7 3.2 copy-start.3
  205.1 8.4 %copy-start.4 = (bf16[8,256,1,2,128]{4,1,3,0,2:T(8,128)(2,1)S(1)}, bf16[8,256,1,2,128]{4,1,3,0,2:T(8,128)(2,1)}, u32[]{:S(2)}) copy-start(bf16[8,256,1,2,128]{4,1,3,0,2:T(8,128)(2,1)} %fusion.6) | copy-start | bytes 3145732
  333.4 2.6 copy-start
  341.7 160.0 %reduce-scatter.3.cloned.1.call-start = ((), (), s32[]{:S(2)}) async-start(), calls=%async_computation.5 | async-start | bytes 8912896 | tf_op jit(solution)/shard_map/reduce_scatter | solution.py:107
Sparse Core Ops, SparseCore 0:
  10.4 65.2 all-gather.2
  341.8 67.5 reduce-scatter.4
  413.1 88.5 reduce-scatter.2
where the time goes:
time: 511 us; the launch traced here: 510 us
  waiting for transfers between devices  276 us (54%)
  blocking collectives  119 us (23%)
  matrix products  43 us (8%)
  local copies, waits for them, and re-layouts  41.6 us (8%)
  between operations  13.9 us (3%)
  other arithmetic  8.63 us (2%)
  starting transfers between devices  7.64 us (1%)
    all_to_all x1, blocking collectives, body(): lax.all_to_all(return_buf.reshape(dp_count, capacity, NL, 2 * head_cols),...  99.2 us
    all_to_all x1, waiting for transfers between devices, body(): lax.all_to_all(outgoing, 'dp', split_axis=0, concat_axis=0, tiled=True)  92.9 us
    reduce_scatter x1, waiting for transfers between devices, body(): lax.psum_scatter(width_terms, 'mp', scatter_dimension=1, tiled=True)  89.6 us
    reduce_scatter x1, waiting for transfers between devices, body(): lax.psum_scatter(lax.dot_general(whole_enc, block_grad, contract_rows, pr...  50.9 us
    all_gather x1, waiting for transfers between devices, body(): whole_enc = lax.all_gather(encoded, 'mp', axis=1, tiled=True)  41.6 us
    all_gather x1, blocking collectives, body(): lax.all_gather(nbr_ids, 'dp', axis=0, tiled=True)  20.2 us
  transfers between devices with their start and end apart: 4, of which 4 were waited for; matrix products, arithmetic and copies ran while one was open for 5% of the time, Pallas kernels for 0%

commit v1 on v0

v1 whole, which is shorter than its diff:
```python
import math

import jax
import jax.numpy as jnp
from jax import lax
from jax.experimental import pallas as pl
from jax.experimental.pallas import tpu as pltpu
from jax.sharding import PartitionSpec as P

HD = 128
SPAN = 64
NL = 128
K = 2
NB_DEV = 4
DP = 16
MP = 16
ZN = 8
SIDE = 4
SHARD = 256
ROWS = 512
HALF = 256
CHUNK = 128
SLOTS = 32
MESH = pl.DeviceIdType.MESH
SCALE = 1.0 / math.sqrt(HD)
OFFSETS = (0, -1, 1, 2)
NT = (((1,), (1,)), ((), ()))
NN = (((1,), (0,)), ((), ()))
TN = (((0,), (0,)), ((), ()))


def dot(a, b, dims):
    return lax.dot_general(a, b, dims, preferred_element_type=jnp.float32)


def wrap(value, size):
    return lax.rem(value + size, size)


class Place:
    def __init__(self):
        self.dp = lax.axis_index("dp")
        self.mp = lax.axis_index("mp")
        self.z, self.core = lax.div(self.dp, 2), lax.rem(self.dp, 2)
        self.x, self.y = lax.div(self.mp, SIDE), lax.rem(self.mp, SIDE)
        self.sibling = self.z * 2 + 1 - self.core

    def along_z(self, step, other_core=False):
        core = 1 - self.core if other_core else self.core
        return wrap(self.z + step, ZN) * 2 + core

    def in_plane(self, path, first, second):
        along_x, along_y = (first, second) if path == 0 else (second, first)
        return wrap(self.x + along_x, SIDE) * SIDE + wrap(self.y + along_y, SIDE)

    def plane_neighbour(self, path, axis, way):
        step = 1 if way == 0 else -1
        return self.in_plane(path, step, 0) if axis == 0 else self.in_plane(path, 0, step)

    def z_device(self, way):
        return (self.along_z(1 if way == 0 else -1), self.mp)

    def greet(self, plane=True):
        others = [self.z_device(0), self.z_device(1), (self.sibling, self.mp)]
        if plane:
            others += [(self.dp, self.plane_neighbour(0, axis, way)) for axis in (0, 1) for way in (0, 1)]
        barrier = pltpu.get_barrier_semaphore()
        for device in others:
            pl.semaphore_signal(barrier, inc=1, device_id=device, device_id_type=MESH)
        pl.semaphore_wait(barrier, len(others))


class Sends:
    def __init__(self):
        self.started = []

    def send(self, src, dst, send_sem, recv_sem, device):
        copy = pltpu.make_async_remote_copy(
            src_ref=src,
            dst_ref=dst,
            send_sem=send_sem,
            recv_sem=recv_sem,
            device_id=device,
            device_id_type=MESH,
        )
        copy.start()
        self.started.append(copy)

    def finish(self):
        for copy in self.started:
            copy.wait_send()


def landed(ref, sem):
    pltpu.make_async_copy(ref, ref, sem).wait()


def gather_kernel(
    q_ref, g_ref, e_ref, ids_ref, kw_ref, vw_ref,
    q_all, g_all, enc_out, kv_ref, ids_all,
    enc, kw, vw, acc, local_sem, zs, zr, cs, cr, p1s, p1r, p2s, p2r,
):
    at = Place()
    out = Sends()
    srcs, alls = (q_ref, g_ref, ids_ref), (q_all, g_all, ids_all)
    at.greet()

    def z_send(way, step, kind):
        origin = at.along_z(1 - step if way == 0 else step - 1)
        src = srcs[kind] if step == 1 else alls[kind].at[origin]
        out.send(src, alls[kind].at[origin], zs.at[way, step - 1, kind], zr.at[way, step - 1, kind], at.z_device(way))

    def core_send(which, kind, origin, src):
        out.send(src, alls[kind].at[origin], cs.at[which, kind], cr.at[which, kind], (at.sibling, at.mp))

    def carries(way, step, kind):
        return step < 4 or (step == 4 and (way == 1) == (kind == 1))

    def z_arrive(way, step, kind):
        origin = at.along_z(-step if way == 0 else step)
        landed(alls[kind].at[origin], zr.at[way, step - 1, kind])
        if carries(way, step + 1, kind):
            z_send(way, step + 1, kind)
        core_send(way * 4 + step, kind, origin, alls[kind].at[origin])

    def rows_of(path):
        return pl.ds(path * HALF, HALF)

    def part_of(path, way):
        return pl.ds(path * HALF + way * CHUNK, CHUNK)

    def p2_first(path, k):
        origin = at.in_plane(path, OFFSETS[k], 0)
        dst = enc.at[origin, rows_of(path)]
        src = e_ref.at[rows_of(path)] if k == 0 else dst
        for way in (0, 1):
            device = (at.dp, at.plane_neighbour(path, 1, way))
            out.send(src, dst, p2s.at[path, k, way], p2r.at[path, k, way], device)

    def p1_first(path):
        for way in (0, 1):
            device = (at.dp, at.plane_neighbour(path, 0, way))
            out.send(
                e_ref.at[rows_of(path)], enc.at[at.mp, rows_of(path)],
                p1s.at[path, way], p1r.at[path, way], device,
            )

    def p1_arrive(path, way):
        origin = at.in_plane(path, -1 if way == 0 else 1, 0)
        landed(enc.at[origin, rows_of(path)], p1r.at[path, way])
        part = enc.at[origin, part_of(path, way)]
        device = (at.dp, at.plane_neighbour(path, 0, way))
        out.send(part, part, p1s.at[path, 2 + way], p1r.at[path, 2 + way], device)
        p2_first(path, 1 + way)

    def p1_far(path):
        origin = at.in_plane(path, 2, 0)
        for way in (0, 1):
            landed(enc.at[origin, part_of(path, way)], p1r.at[path, 2 + way])
        p2_first(path, 3)

    def p2_arrive(path, k):
        for way in (0, 1):
            origin = at.in_plane(path, OFFSETS[k], -1 if way == 0 else 1)
            landed(enc.at[origin, rows_of(path)], p2r.at[path, k, way])
            part = enc.at[origin, part_of(path, way)]
            device = (at.dp, at.plane_neighbour(path, 1, way))
            out.send(part, part, p2s.at[path, k, 2 + way], p2r.at[path, k, 2 + way], device)

    def p2_far(path, k):
        origin = at.in_plane(path, OFFSETS[k], 2)
        for way in (0, 1):
            landed(enc.at[origin, part_of(path, way)], p2r.at[path, k, 2 + way])

    def project(batch):
        def one(j, carry):
            rows = pl.ds(pl.multiple_of(j * SHARD, SHARD), SHARD)
            block = enc[j]
            acc[:, :SHARD] += dot(block, kw[rows, :], NN)
            acc[:, SHARD:] += dot(block, vw[rows, :], NN)
            return carry

        lax.fori_loop(batch * 4, batch * 4 + 4, one, 0)

    for way in (0, 1):
        z_send(way, 1, 2)
    for kind in (0, 1):
        for way in (0, 1):
            z_send(way, 1, kind)
    for path in (0, 1):
        p1_first(path)
    for path in (0, 1):
        p2_first(path, 0)
    for kind in (2, 0, 1):
        core_send(0, kind, at.dp, srcs[kind])
    locals_ = [
        pltpu.make_async_copy(e_ref, enc.at[at.mp], local_sem.at[0]),
        pltpu.make_async_copy(kw_ref, kw, local_sem.at[1]),
        pltpu.make_async_copy(vw_ref, vw, local_sem.at[2]),
        pltpu.make_async_copy(q_ref, q_all.at[at.dp], local_sem.at[3]),
        pltpu.make_async_copy(g_ref, g_all.at[at.dp], local_sem.at[4]),
        pltpu.make_async_copy(ids_ref, ids_all.at[at.dp], local_sem.at[5]),
    ]
    for copy in locals_:
        copy.start()
    acc[...] = jnp.zeros_like(acc)

    for way in (0, 1):
        for path in (0, 1):
            p1_arrive(path, way)
    for way in (0, 1):
        z_arrive(way, 1, 2)
    for path in (0, 1):
        p2_arrive(path, 0)
    for way in (0, 1):
        z_arrive(way, 1, 0)
    for path in (0, 1):
        p1_far(path)
    for way in (0, 1):
        z_arrive(way, 2, 2)
    for path in (0, 1):
        p2_arrive(path, 1)
    for way in (0, 1):
        z_arrive(way, 1, 1)
    for path in (0, 1):
        p2_arrive(path, 2)
    for way in (0, 1):
        z_arrive(way, 3, 2)
    for way in (0, 1):
        z_arrive(way, 2, 0)
    for path in (0, 1):
        p2_arrive(path, 3)
    for k in range(4):
        for path in (0, 1):
            p2_far(path, k)
    for copy in locals_:
        copy.wait()
    write_enc = pltpu.make_async_copy(enc, enc_out, local_sem.at[0])
    write_enc.start()
    for way in (0, 1):
        z_arrive(way, 2, 1)
    project(0)
    z_arrive(0, 4, 2)
    for way in (0, 1):
        z_arrive(way, 3, 0)
    project(1)
    for way in (0, 1):
        z_arrive(way, 3, 1)
    project(2)
    project(3)
    kv_ref[...] = acc[...].astype(jnp.bfloat16)
    z_arrive(0, 4, 0)
    z_arrive(1, 4, 1)
    for kind in (0, 1, 2):
        landed(alls[kind].at[at.sibling], cr.at[0, kind])
        for way in (0, 1):
            for step in range(1, 5):
                if carries(way, step, kind):
                    origin = at.along_z(-step if way == 0 else step, other_core=True)
                    landed(alls[kind].at[origin], cr.at[way * 4 + step, kind])
    write_enc.wait()
    out.finish()


def gather(queries, grad_attn, encoded, ids, key_weight, value_weight):
    any_ = pl.BlockSpec(memory_space=pl.ANY)
    vmem = pl.BlockSpec(memory_space=pltpu.VMEM)
    dma = pltpu.SemaphoreType.DMA
    bf16 = jnp.bfloat16
    return pl.pallas_call(
        gather_kernel,
        out_shape=(
            jax.ShapeDtypeStruct((DP, ROWS, SHARD), bf16),
            jax.ShapeDtypeStruct((DP, ROWS, SHARD), bf16),
            jax.ShapeDtypeStruct((MP, ROWS, SHARD), bf16),
            jax.ShapeDtypeStruct((ROWS, 2 * SHARD), bf16),
            jax.ShapeDtypeStruct((DP, 8, 128), jnp.int32),
        ),
        in_specs=[any_, any_, any_, vmem, any_, any_],
        out_specs=(any_, any_, any_, vmem, vmem),
        scratch_shapes=[
            pltpu.VMEM((MP, ROWS, SHARD), bf16),
            pltpu.VMEM((MP * SHARD, SHARD), bf16),
            pltpu.VMEM((MP * SHARD, SHARD), bf16),
            pltpu.VMEM((ROWS, 2 * SHARD), jnp.float32),
            dma((6,)),
            dma((2, 4, 3)), dma((2, 4, 3)),
            dma((9, 3)), dma((9, 3)),
            dma((2, 4)), dma((2, 4)),
            dma((2, 4, 4)), dma((2, 4, 4)),
        ],
        compiler_params=pltpu.CompilerParams(
            collective_id=0, has_side_effects=True, vmem_limit_bytes=40 * 2**20
        ),
        name="gather_all",
    )(queries, grad_attn, encoded, ids, key_weight, value_weight)


def fetch_slots(table, q_all, g_all, qs, gs, sem):
    def issue(p, carry):
        rows = pl.ds(pl.multiple_of(table[p] * SPAN, SPAN), SPAN)
        to = pl.ds(pl.multiple_of(p * SPAN, SPAN), SPAN)
        requester = lax.div(p, 2)
        pltpu.make_async_copy(q_all.at[requester, rows], qs.at[to], sem.at[0]).start()
        pltpu.make_async_copy(g_all.at[requester, rows], gs.at[to], sem.at[1]).start()
        return carry

    lax.fori_loop(0, SLOTS, issue, 0)
    landed(qs, sem.at[0])
    landed(gs, sem.at[1])


def block_rows(table, p):
    return pl.ds(pl.multiple_of(table[SLOTS + p] * NL, NL), NL)


def slot_products(kv, blocks, head, q_rows, g_rows, first):
    cols = slice(head * HD, (head + 1) * HD)
    vcols = slice(SHARD + head * HD, SHARD + (head + 1) * HD)
    qh, gh = q_rows[:, cols], g_rows[:, cols]
    keys = [kv[rows, cols] for rows in blocks]
    values = [kv[rows, vcols] for rows in blocks]
    scores = jnp.where(first, dot(keys[0], qh, NT), dot(keys[1], qh, NT)) * SCALE
    prob_grad = jnp.where(first, dot(values[0], gh, NT), dot(values[1], gh, NT))
    return qh, gh, keys, scores, prob_grad


def stats_kernel(table, q_all, g_all, kv, stats, qs, gs, sem):
    fetch_slots(table, q_all, g_all, qs, gs, sem)
    first = lax.broadcasted_iota(jnp.int32, (NL, 2 * SPAN), 1) < SPAN

    def one(i, carry):
        rows = pl.ds(pl.multiple_of(i * 2 * SPAN, 2 * SPAN), 2 * SPAN)
        q_rows, g_rows = qs[rows, :], gs[rows, :]
        blocks = [block_rows(table, 2 * i), block_rows(table, 2 * i + 1)]
        for head in (0, 1):
            _, _, _, scores, prob_grad = slot_products(kv, blocks, head, q_rows, g_rows, first)
            top = jnp.max(scores, axis=0, keepdims=True)
            e = jnp.exp(scores - top)
            total = jnp.sum(e, axis=0, keepdims=True)
            stats[pl.ds(i * 4 + head, 1), :] = top + jnp.log(total)
            stats[pl.ds(i * 4 + 2 + head, 1), :] = jnp.sum(e * prob_grad, axis=0, keepdims=True) / total
        return carry

    lax.fori_loop(0, DP, one, 0)


def slot_stats(table, q_all, g_all, kv):
    any_ = pl.BlockSpec(memory_space=pl.ANY)
    vmem = pl.BlockSpec(memory_space=pltpu.VMEM)
    return pl.pallas_call(
        stats_kernel,
        out_shape=jax.ShapeDtypeStruct((DP * 4, 128), jnp.float32),
        in_specs=[pl.BlockSpec(memory_space=pltpu.SMEM), any_, any_, vmem],
        out_specs=vmem,
        scratch_shapes=[
            pltpu.VMEM((SLOTS * SPAN, SHARD), jnp.bfloat16),
            pltpu.VMEM((SLOTS * SPAN, SHARD), jnp.bfloat16),
            pltpu.SemaphoreType.DMA((2,)),
        ],
        compiler_params=pltpu.CompilerParams(vmem_limit_bytes=40 * 2**20),
        name="slot_stats",
    )(table, q_all, g_all, kv)


def share_kernel(stats, all_stats, local_sem, zs, zr, cs, cr):
    at = Place()
    out = Sends()
    at.greet(plane=False)

    def z_send(way, step):
        origin = at.along_z(1 - step if way == 0 else step - 1)
        src = stats if step == 1 else all_stats.at[origin]
        out.send(src, all_stats.at[origin], zs.at[way, step - 1], zr.at[way, step - 1], at.z_device(way))

    def core_send(which, origin, src):
        out.send(src, all_stats.at[origin], cs.at[which], cr.at[which], (at.sibling, at.mp))

    for way in (0, 1):
        z_send(way, 1)
    core_send(0, at.dp, stats)
    own = pltpu.make_async_copy(stats, all_stats.at[at.dp], local_sem.at[0])
    own.start()
    for step in range(1, 5):
        for way in (0, 1):
            if step == 4 and way == 1:
                continue
            origin = at.along_z(-step if way == 0 else step)
            landed(all_stats.at[origin], zr.at[way, step - 1])
            if step < 3 or (step == 3 and way == 0):
                z_send(way, step + 1)
            core_send(way * 4 + step, origin, all_stats.at[origin])
    own.wait()
    landed(all_stats.at[at.sibling], cr.at[0])
    for step in range(1, 5):
        for way in (0, 1):
            if step == 4 and way == 1:
                continue
            origin = at.along_z(-step if way == 0 else step, other_core=True)
            landed(all_stats.at[origin], cr.at[way * 4 + step])
    out.finish()


def share_stats(stats):
    vmem = pl.BlockSpec(memory_space=pltpu.VMEM)
    dma = pltpu.SemaphoreType.DMA
    return pl.pallas_call(
        share_kernel,
        out_shape=jax.ShapeDtypeStruct((DP, DP * 4, 128), jnp.float32),
        in_specs=[vmem],
        out_specs=vmem,
        scratch_shapes=[dma((1,)), dma((2, 4)), dma((2, 4)), dma((9,)), dma((9,))],
        compiler_params=pltpu.CompilerParams(
            collective_id=1, has_side_effects=True, vmem_limit_bytes=40 * 2**20
        ),
        name="share_stats",
    )(stats)


def grads_kernel(table, q_all, g_all, kv, all_stats, block_grad, dq, qs, gs, acc, sem):
    def clear(i, carry):
        dq[i] = jnp.zeros((ROWS, SHARD), jnp.bfloat16)
        return carry

    fetch_slots(table, q_all, g_all, qs, gs, sem)
    lax.fori_loop(0, DP, clear, 0)
    acc[...] = jnp.zeros_like(acc)
    me = table[5 * SLOTS]
    lanes = lax.broadcasted_iota(jnp.int32, (NL, 2 * SPAN), 1)
    first = lanes < SPAN
    first_row = lax.broadcasted_iota(jnp.int32, (1, 2 * SPAN), 1) < SPAN

    def one(i, carry):
        rows = pl.ds(pl.multiple_of(i * 2 * SPAN, 2 * SPAN), 2 * SPAN)
        q_rows, g_rows = qs[rows, :], gs[rows, :]
        blocks = [block_rows(table, 2 * i), block_rows(table, 2 * i + 1)]
        filled = [table[4 * SLOTS + 2 * i + rank] for rank in (0, 1)]
        keep = jnp.where(first, filled[0], filled[1]) > 0

        def partner(stat):
            found = []
            for rank in (0, 1):
                owner = table[2 * SLOTS + 2 * i + rank]
                there = table[3 * SLOTS + 2 * i + rank]
                row = all_stats[owner, pl.ds(i * 4 + stat, 1), :]
                found.append(jnp.where(there == rank, row, pltpu.roll(row, SPAN, 1)))
            return jnp.where(first_row, found[0], found[1])

        for head in (0, 1):
            cols = slice(head * HD, (head + 1) * HD)
            vcols = slice(SHARD + head * HD, SHARD + (head + 1) * HD)
            qh, gh, keys, scores, prob_grad = slot_products(kv, blocks, head, q_rows, g_rows, first)
            lse_here = all_stats[me, pl.ds(i * 4 + head, 1), :]
            lse_there = partner(head)
            delta_here = all_stats[me, pl.ds(i * 4 + 2 + head, 1), :]
            delta_there = partner(2 + head)
            top = jnp.maximum(lse_here, lse_there)
            lse = top + jnp.log(jnp.exp(lse_here - top) + jnp.exp(lse_there - top))
            delta = jnp.exp(lse_here - lse) * delta_here + jnp.exp(lse_there - lse) * delta_there
            prob = jnp.exp(scores - lse)
            score_grad = prob * (prob_grad - delta) * SCALE
            zero = jnp.zeros_like(prob)
            prob = jnp.where(keep, prob, zero)
            score_grad = jnp.where(keep, score_grad, zero)
            parts = [(first, 0), (jnp.logical_not(first), 1)]
            for mask, rank in parts:
                ds = jnp.where(mask, score_grad, zero).astype(jnp.bfloat16)
                pr = jnp.where(mask, prob, zero).astype(jnp.bfloat16)
                acc[blocks[rank], cols] += dot(ds, qh, NN)
                acc[blocks[rank], vcols] += dot(pr, gh, NN)
                span = table[2 * i + rank]
                where = pl.ds(pl.multiple_of(span * SPAN, SPAN), SPAN)
                dq_rows = dot(ds, keys[rank], TN)[rank * SPAN : (rank + 1) * SPAN, :]
                old = dq[i, where, cols].astype(jnp.float32)
                dq[i, where, cols] = (old + dq_rows).astype(jnp.bfloat16)
        return carry

    lax.fori_loop(0, DP, one, 0)
    block_grad[...] = acc[...].astype(jnp.bfloat16)


def slot_grads(table, q_all, g_all, kv, all_stats):
    any_ = pl.BlockSpec(memory_space=pl.ANY)
    vmem = pl.BlockSpec(memory_space=pltpu.VMEM)
    return pl.pallas_call(
        grads_kernel,
        out_shape=(
            jax.ShapeDtypeStruct((ROWS, 2 * SHARD), jnp.bfloat16),
            jax.ShapeDtypeStruct((DP, ROWS, SHARD), jnp.bfloat16),
        ),
        in_specs=[pl.BlockSpec(memory_space=pltpu.SMEM), any_, any_, vmem, vmem],
        out_specs=(vmem, vmem),
        scratch_shapes=[
            pltpu.VMEM((SLOTS * SPAN, SHARD), jnp.bfloat16),
            pltpu.VMEM((SLOTS * SPAN, SHARD), jnp.bfloat16),
            pltpu.VMEM((ROWS, 2 * SHARD), jnp.float32),
            pltpu.SemaphoreType.DMA((2,)),
        ],
        compiler_params=pltpu.CompilerParams(vmem_limit_bytes=40 * 2**20),
        name="slot_grads",
    )(table, q_all, g_all, kv, all_stats)


def reduce_kernel(
    bg, enc_ref, kw_ref, vw_ref, dq_ref,
    dq_out, eg_out, kg_out, vg_out,
    enc, kw, vw, own_dq, zsb, zrb, csb, crb, xs1, xr1, xs2, xr2, group, ys1, yr1, ys2, yr2,
    local_sem, zs, zr, cs, cr, x1s, x1r, x2s, x2r, y1s, y1r, y2s, y2r,
):
    at = Place()
    out = Sends()
    bf16 = jnp.bfloat16

    loads = [
        pltpu.make_async_copy(enc_ref, enc, local_sem.at[0]),
        pltpu.make_async_copy(kw_ref, kw, local_sem.at[1]),
        pltpu.make_async_copy(vw_ref, vw, local_sem.at[2]),
    ]
    for copy in loads:
        copy.start()
    own_loads = []
    for j in range(ZN):
        own_loads.append(pltpu.make_async_copy(dq_ref.at[j * 2 + at.core], own_dq.at[j], local_sem.at[3 + j]))
        own_loads[-1].start()
    at.greet()

    order = (4, 3, -3, 2, -2, 1, -1, 0)

    def core_send(kind, which):
        target = wrap(at.z + order[which], ZN)
        device = (at.sibling, at.mp)
        src = dq_ref.at[target * 2 + 1 - at.core] if kind == 0 else csb.at[target]
        out.send(src, crb.at[kind, target], cs.at[kind, which], cr.at[kind, which], device)

    def weight_part(index):
        block = enc[index]
        return [dot(block, bg[:, col * SHARD : (col + 1) * SHARD], TN) for col in (0, 1)]

    def weight_for_sibling(which):
        target = wrap(at.z + order[which], ZN)
        parts = weight_part(target * 2 + 1 - at.core)
        for col in (0, 1):
            csb[target, pl.ds(col * HALF, HALF), :] = parts[col].astype(bf16)
        core_send(1, which)

    def term(kind, which, half):
        target = wrap(at.z + order[which], ZN)
        rows = pl.ds(half * HALF, HALF)
        if kind == 0:
            mine = own_dq[target, rows, :].astype(jnp.float32)
        else:
            mine = dot(enc[target * 2 + at.core], bg[:, half * SHARD : (half + 1) * SHARD], TN)
        return mine + crb[kind, target, rows, :].astype(jnp.float32)

    def z_region(step, way):
        return pl.ds(way * HALF, HALF) if step == 1 else pl.ds(0, ROWS)

    def z_step(kind, way, step):
        which = 0 if step == 1 else 2 * step - 3 + way
        target = wrap(at.z + order[which], ZN)
        if step > 1 or way == 0:
            landed(crb.at[kind, target], cr.at[kind, which])
        if step > 1:
            region = z_region(step - 1, way)
            landed(zrb.at[kind, way, step - 2, region], zr.at[kind, way, step - 2])
        for half in (0, 1):
            if step == 1 and half != way:
                continue
            rows = pl.ds(half * HALF, HALF)
            value = term(kind, which, half)
            if step > 2 or (step == 2 and half == way):
                value = value + zrb[kind, way, step - 2, rows, :].astype(jnp.float32)
            zsb[kind, way, step - 1, rows, :] = value.astype(bf16)
        region = z_region(step, way)
        out.send(
            zsb.at[kind, way, step - 1, region], zrb.at[kind, way, step - 1, region],
            zs.at[kind, way, step - 1], zr.at[kind, way, step - 1], at.z_device(way),
        )

    def z_final(kind):
        landed(crb.at[kind, at.z], cr.at[kind, 7])
        for way in (0, 1):
            landed(zrb.at[kind, way, 3], zr.at[kind, way, 3])
        for half in (0, 1):
            rows = pl.ds(half * HALF, HALF)
            value = term(kind, 7, half)
            for way in (0, 1):
                value = value + zrb[kind, way, 3, rows, :].astype(jnp.float32)
            if kind == 0:
                dq_out[rows, :] = value.astype(bf16)
            elif half == 0:
                kg_out[...] = value
            else:
                vg_out[...] = value

    def width_index(path, offset, j):
        if path == 0:
            return wrap(at.x + offset, SIDE) * SIDE + j
        return j * SIDE + wrap(at.y + offset, SIDE)

    def width_part(path, start, size, offset, j):
        rows = pl.ds(path * HALF + start, size)
        cols = pl.ds(pl.multiple_of(width_index(path, offset, j) * SHARD, SHARD), SHARD)
        return dot(bg[rows, :SHARD], kw[cols, :], NT) + dot(bg[rows, SHARD:], vw[cols, :], NT)

    def width_far(path):
        def one(j, carry):
            value = width_part(path, 0, HALF, 2, j).astype(bf16)
            for way in (0, 1):
                xs1[path, way, j] = value[way * CHUNK : (way + 1) * CHUNK, :]
            return carry

        lax.fori_loop(0, SIDE, one, 0)
        for way in (0, 1):
            device = (at.dp, at.plane_neighbour(path, 0, way))
            out.send(xs1.at[path, way], xr1.at[path, way], x1s.at[path, way], x1r.at[path, way], device)

    def width_near(path, way):
        landed(xr1.at[path, way], x1r.at[path, way])

        def one(j, carry):
            value = width_part(path, 0, HALF, 1 if way == 0 else -1, j)
            came = xr1[path, way, j].astype(jnp.float32)
            for part in (0, 1):
                piece = value[part * CHUNK : (part + 1) * CHUNK, :]
                piece = piece + came if part == way else piece
                xs2[path, way, j, pl.ds(part * CHUNK, CHUNK), :] = piece.astype(bf16)
            return carry

        lax.fori_loop(0, SIDE, one, 0)
        device = (at.dp, at.plane_neighbour(path, 0, way))
        out.send(xs2.at[path, way], xr2.at[path, way], x2s.at[path, way], x2r.at[path, way], device)

    def second(path):
        return at.y if path == 0 else at.x

    def width_own(path):
        for way in (0, 1):
            landed(xr2.at[path, way], x2r.at[path, way])

        def one(j, carry):
            value = width_part(path, 0, HALF, 0, j)
            for way in (0, 1):
                value = value + xr2[path, way, j].astype(jnp.float32)
            group[path, j] = value
            return carry

        lax.fori_loop(0, SIDE, one, 0)
        far = wrap(second(path) + 2, SIDE)
        for way in (0, 1):
            ys1[path, way] = group[path, far, pl.ds(way * CHUNK, CHUNK), :].astype(bf16)
            device = (at.dp, at.plane_neighbour(path, 1, way))
            out.send(ys1.at[path, way], yr1.at[path, way], y1s.at[path, way], y1r.at[path, way], device)

    def width_second(path):
        for way in (0, 1):
            landed(yr1.at[path, way], y1r.at[path, way])
            near = wrap(second(path) + (1 if way == 0 else -1), SIDE)
            for part in (0, 1):
                piece = group[path, near, pl.ds(part * CHUNK, CHUNK), :]
                if part == way:
                    piece = piece + yr1[path, way].astype(jnp.float32)
                ys2[path, way, pl.ds(part * CHUNK, CHUNK), :] = piece.astype(bf16)
            device = (at.dp, at.plane_neighbour(path, 1, way))
            out.send(ys2.at[path, way], yr2.at[path, way], y2s.at[path, way], y2r.at[path, way], device)

    def width_final(path):
        value = group[path, second(path)]
        for way in (0, 1):
            landed(yr2.at[path, way], y2r.at[path, way])
            value = value + yr2[path, way].astype(jnp.float32)
        eg_out[pl.ds(path * HALF, HALF), :] = value.astype(bf16)

    for which in range(ZN):
        core_send(0, which)
    loads[0].wait()
    weight_for_sibling(0)
    for copy in own_loads:
        copy.wait()
    for way in (0, 1):
        z_step(0, way, 1)
    loads[1].wait()
    loads[2].wait()
    for path in (0, 1):
        width_far(path)
    for way in (0, 1):
        z_step(1, way, 1)
    weight_for_sibling(1)
    weight_for_sibling(2)
    for way in (0, 1):
        z_step(0, way, 2)
    for way in (0, 1):
        for path in (0, 1):
            width_near(path, way)
    for way in (0, 1):
        z_step(1, way, 2)
    weight_for_sibling(3)
    weight_for_sibling(4)
    for way in (0, 1):
        z_step(0, way, 3)
    for path in (0, 1):
        width_own(path)
    for way in (0, 1):
        z_step(1, way, 3)
    for which in (5, 6, 7):
        weight_for_sibling(which)
    for path in (0, 1):
        width_second(path)
    for way in (0, 1):
        z_step(0, way, 4)
    for path in (0, 1):
        width_final(path)
    for way in (0, 1):
        z_step(1, way, 4)
    z_final(0)
    z_final(1)
    out.finish()


def reduce_all(block_grad, enc_all, key_weight, value_weight, dq):
    any_ = pl.BlockSpec(memory_space=pl.ANY)
    vmem = pl.BlockSpec(memory_space=pltpu.VMEM)
    dma = pltpu.SemaphoreType.DMA
    bf16, f32 = jnp.bfloat16, jnp.float32
    return pl.pallas_call(
        reduce_kernel,
        out_shape=(
            jax.ShapeDtypeStruct((ROWS, SHARD), bf16),
            jax.ShapeDtypeStruct((ROWS, SHARD), bf16),
            jax.ShapeDtypeStruct((SHARD, SHARD), f32),
            jax.ShapeDtypeStruct((SHARD, SHARD), f32),
        ),
        in_specs=[vmem, any_, any_, any_, any_],
        out_specs=(vmem, vmem, vmem, vmem),
        scratch_shapes=[
            pltpu.VMEM((MP, ROWS, SHARD), bf16),
            pltpu.VMEM((MP * SHARD, SHARD), bf16),
            pltpu.VMEM((MP * SHARD, SHARD), bf16),
            pltpu.VMEM((ZN, ROWS, SHARD), bf16),
            pltpu.VMEM((2, 2, 4, ROWS, SHARD), bf16),
            pltpu.VMEM((2, 2, 4, ROWS, SHARD), bf16),
            pltpu.VMEM((ZN, ROWS, SHARD), bf16),
            pltpu.VMEM((2, ZN, ROWS, SHARD), bf16),
            pltpu.VMEM((2, 2, SIDE, CHUNK, SHARD), bf16),
            pltpu.VMEM((2, 2, SIDE, CHUNK, SHARD), bf16),
            pltpu.VMEM((2, 2, SIDE, HALF, SHARD), bf16),
            pltpu.VMEM((2, 2, SIDE, HALF, SHARD), bf16),
            pltpu.VMEM((2, SIDE, HALF, SHARD), f32),
            pltpu.VMEM((2, 2, CHUNK, SHARD), bf16),
            pltpu.VMEM((2, 2, CHUNK, SHARD), bf16),
            pltpu.VMEM((2, 2, HALF, SHARD), bf16),
            pltpu.VMEM((2, 2, HALF, SHARD), bf16),
            dma((3 + ZN,)),
            dma((2, 2, 4)), dma((2, 2, 4)),
            dma((2, ZN)), dma((2, ZN)),
            dma((2, 2)), dma((2, 2)),
            dma((2, 2)), dma((2, 2)),
            dma((2, 2)), dma((2, 2)),
            dma((2, 2)), dma((2, 2)),
        ],
        compiler_params=pltpu.CompilerParams(
            collective_id=2, has_side_effects=True, vmem_limit_bytes=56 * 2**20
        ),
        name="reduce_all",
    )(block_grad, enc_all, key_weight, value_weight, dq)


def slot_table(ids_all):
    ids = ids_all[:, :, :K].reshape(DP, DP)
    me = lax.axis_index("dp")
    owners, local_block = ids // NB_DEV, ids % NB_DEV
    position = jnp.arange(DP, dtype=jnp.int32)
    alike = (owners[:, :, None] == owners[:, None, :]) & (position[None, :] < position[:, None])
    ranks = jnp.sum(alike.astype(jnp.int32), axis=-1)

    def other(values):
        return values.reshape(DP, DP // K, K)[:, :, ::-1].reshape(DP, DP)

    matched = (owners == me)[:, :, None] & (ranks[:, :, None] == jnp.arange(2, dtype=jnp.int32))
    columns = [
        jnp.broadcast_to(position // K, (DP, DP)), local_block,
        other(owners), other(ranks), jnp.ones((DP, DP), jnp.int32),
    ]
    picked = [jnp.sum(jnp.where(matched, c[:, :, None], 0), axis=1).reshape(-1) for c in columns]
    return jnp.concatenate(picked + [jnp.full((32,), me, jnp.int32)])


def body(queries, grad_attn, encoded, key_weight, value_weight, nbr_ids):
    ids = jnp.pad(nbr_ids, ((0, 0), (0, 128 - K)))
    q_all, g_all, enc_all, kv, ids_all = gather(
        queries, grad_attn, encoded, ids, key_weight, value_weight
    )
    table = slot_table(ids_all)
    stats = slot_stats(table, q_all, g_all, kv)
    all_stats = share_stats(stats)
    block_grad, dq = slot_grads(table, q_all, g_all, kv, all_stats)
    return reduce_all(block_grad, enc_all, key_weight, value_weight, dq)


def solution(mesh):
    return jax.shard_map(
        body,
        mesh=mesh,
        in_specs=(
            P("dp", "mp"),
            P("dp", "mp"),
            P("dp", "mp"),
            P(None, "mp"),
            P(None, "mp"),
            P("dp", None),
        ),
        out_specs=(P("dp", "mp"), P("dp", "mp"), P("dp", "mp"), P("dp", "mp")),
        check_vma=False,
    )
```

time: 511 us -> 175 us (0.34)
  waiting for transfers between devices: 276 us -> 0 us
  Pallas kernels: 0 us -> 146 us
  blocking collectives: 119 us -> 0 us
  matrix products: 43 us -> 0 us
  local copies, waits for them, and re-layouts: 41.6 us -> 26.4 us
  between operations: 13.9 us -> 0.77 us
  other arithmetic: 8.63 us -> 0.78 us
  starting transfers between devices: 7.64 us -> 0 us
    pallas_call x0 -> x5, Pallas kernels: none -> 146 us  [the longest x1 54.2 us: reduce_all(): pl.pallas_call(reduce_kernel, out_shape=(jax.ShapeDtypeStruct((ROWS, SHAR...]
    reduce_scatter x2 -> x0, waiting for transfers between devices: 140 us -> none  [the longest x1 89.6 us: body(): lax.psum_scatter(width_terms, 'mp', scatter_dimension=1, tiled=True)]
    all_to_all x1 -> x0, blocking collectives: 99.2 us -> none  [body(): lax.all_to_all(return_buf.reshape(dp_count, capacity, NL, 2 * head_cols),...]
    all_to_all x1 -> x0, waiting for transfers between devices: 92.9 us -> none  [body(): lax.all_to_all(outgoing, 'dp', split_axis=0, concat_axis=0, tiled=True)]
    dot_general x9 -> x0, matrix products: 43 us -> none  [the longest x1 8.42 us: body(): jnp.einsum('chqk,cqhd->ckhd', score_grad, query_blocks, preferred_element...]
    all_gather x1 -> x0, waiting for transfers between devices: 41.6 us -> none  [body(): whole_enc = lax.all_gather(encoded, 'mp', axis=1, tiled=True)]
    unnamed x19 -> x29, local copies, waits for them, and re-layouts: 3.98 us -> 24.6 us
    all_gather x1 -> x0, blocking collectives: 20.2 us -> none  [body(): lax.all_gather(nbr_ids, 'dp', axis=0, tiled=True)]
  transfers between devices with their start and end apart: 4 -> 0, of which waited for: 4 -> 0; matrix products, arithmetic and copies ran while one was open for 5% -> 0% of each run, Pallas kernels for 0% -> 0%
where the time goes in v1:
time: 175 us; the launch traced here: 174 us
  Pallas kernels  146 us (83%)
  local copies, waits for them, and re-layouts  26.4 us (15%)
    pallas_call x1, Pallas kernels, reduce_all(): pl.pallas_call(reduce_kernel, out_shape=(jax.ShapeDtypeStruct((ROWS, SHAR...  54.2 us
    pallas_call x1, Pallas kernels, gather(): pl.pallas_call(gather_kernel, out_shape=(jax.ShapeDtypeStruct((DP, ROWS,...  52.2 us
    unnamed x29, local copies, waits for them, and re-layouts  24.6 us
    pallas_call x1, Pallas kernels, share_stats(): pl.pallas_call(share_kernel, out_shape=jax.ShapeDtypeStruct((DP, DP * 4,...  15.9 us
    pallas_call x1, Pallas kernels, slot_grads(): pl.pallas_call(grads_kernel, out_shape=(jax.ShapeDtypeStruct((ROWS, 2 * S...  15.5 us
    pallas_call x1, Pallas kernels, slot_stats(): pl.pallas_call(stats_kernel, out_shape=jax.ShapeDtypeStruct((DP * 4, 128)...  8.73 us

profile of v1, /device:TPU:2, one launch (start us, length us, event | category | flops | bytes accessed | tf_op | source)
XLA Modules:
  0.0 174.3 jit_solution(16548053529406397466)
XLA Ops:
  0.7 0.8 copy.21
  1.4 1.6 copy-done.5
  3.0 1.6 copy-done.6
  4.6 0.9 copy-done.9
  5.6 0.9 copy-done.10
  6.5 0.9 copy-done.11
  7.5 52.2 %gather_all.1 = (bf16[16,512,256]{2,1,0:T(8,128)(2,1)S(1)}, bf16[16,512,256]{2,1,0:T(8,128)(2,1)S(1)}, bf16[16,512,256]{2,1,0:T(8,128)(2,1)}, bf16[512,512]{1,0:T(8,128)(2,1)S(1)}, s32[16,8,128]{2,1,0:T(8,128)S(1)}) custom-call(bf16[512,256]{1,0:T(8,128)(2,1)S(1)} %copy-done.9, bf16[512,256]{1,0:T(8,128)(2,1)S(1)} %copy-done.10, ...), custom_call_target="tpu_custom_call" | custom-call | tf_op jit(solution)/shard_map/gather_all/pallas_call | solution.py:270
  59.7 2.0 %copy-done = bf16[16,512,256]{2,1,0:T(8,128)(2,1)} copy-done((bf16[16,512,256]{2,1,0:T(8,128)(2,1)}, bf16[16,512,256]{2,1,0:T(8,128)(2,1)S(1)}, u32[]{:S(2)}) %copy-start) | copy-done | bytes 4194328
  61.6 2.0 %copy-done.3 = bf16[16,512,256]{2,1,0:T(8,128)(2,1)} copy-done((bf16[16,512,256]{2,1,0:T(8,128)(2,1)}, bf16[16,512,256]{2,1,0:T(8,128)(2,1)S(1)}, u32[]{:S(2)}) %copy-start.3) | copy-done | bytes 4194328
  63.7 0.1 copy.29
  63.9 0.1 copy.22
  64.2 0.1 copy.23
  64.3 0.4 convert_reduce_fusion
  64.9 0.3 select_reduce_fusion
  65.3 0.1 reshape.138
  65.5 0.1 reshape.137
  65.6 0.1 copy.31
  65.6 0.1 reshape.135
  65.8 0.1 reshape.134
  66.0 0.1 reshape.133
  66.2 2.2 %copy-done.1 = bf16[16,512,256]{2,1,0:T(8,128)(2,1)S(1)} copy-done((bf16[16,512,256]{2,1,0:T(8,128)(2,1)S(1)}, bf16[16,512,256]{2,1,0:T(8,128)(2,1)}, u32[]{:S(2)}) %copy-start.1) | copy-done | bytes 4194328
  68.4 2.2 %copy-done.4 = bf16[16,512,256]{2,1,0:T(8,128)(2,1)S(1)} copy-done((bf16[16,512,256]{2,1,0:T(8,128)(2,1)S(1)}, bf16[16,512,256]{2,1,0:T(8,128)(2,1)}, u32[]{:S(2)}) %copy-start.4) | copy-done | bytes 4194328
  70.5 8.7 %slot_stats.1.stats = f32[64,128]{1,0:T(8,128)S(1)} custom-call(s32[192]{0:T(256)S(1)} %concatenate.3.table, bf16[16,512,256]{2,1,0:T(8,128)(2,1)S(1)} %copy-done.1, bf16[16,512,256]{2,1,0:T(8,128)(2,1)S(1)} %copy-done.4, bf16[512,512]{1,0:T(8,128)(2,1)S(1)} %get-tuple-element.14.kv), custom_call_target="tpu_custom_call" | custom-call | tf_op jit(solution)/shard_map/slot_stats/pallas_call | solution.py:351
  79.3 15.9 %share_stats.1.all_stats = f32[16,64,128]{2,1,0:T(8,128)S(1)} custom-call(f32[64,128]{1,0:T(8,128)S(1)} %slot_stats.1.stats), custom_call_target="tpu_custom_call" | custom-call | tf_op jit(solution)/shard_map/share_stats/pallas_call | solution.py:407
  95.2 15.5 %slot_grads.1 = (bf16[512,512]{1,0:T(8,128)(2,1)S(1)}, bf16[16,512,256]{2,1,0:T(8,128)(2,1)S(1)}) custom-call(s32[192]{0:T(256)S(1)} %concatenate.3.table, bf16[16,512,256]{2,1,0:T(8,128)(2,1)S(1)} %copy-done.2, bf16[16,512,256]{2,1,0:T(8,128)(2,1)S(1)} %copy-done.4, bf16[512,512]{1,0:T(8,128)(2,1)S(1)} %get-tuple-element.14.kv, ...), custom_call_target="tpu_custom_call" | custom-call | tf_op jit(solution)/shard_map/slot_grads/pallas_call | solution.py:485
  110.6 2.0 %copy-done.7 = bf16[16,512,256]{2,1,0:T(8,128)(2,1)} copy-done((bf16[16,512,256]{2,1,0:T(8,128)(2,1)}, bf16[16,512,256]{2,1,0:T(8,128)(2,1)S(1)}, u32[]{:S(2)}) %copy-start.7) | copy-done | bytes 4194328
  112.6 0.8 copy-done.8
  113.4 54.2 %reduce_all.1 = (bf16[512,256]{1,0:T(8,128)(2,1)}, bf16[512,256]{1,0:T(8,128)(2,1)}, f32[256,256]{1,0:T(8,128)}, f32[256,256]{1,0:T(8,128)}) custom-call(bf16[512,512]{1,0:T(8,128)(2,1)} %copy-done.8, bf16[16,512,256]{2,1,0:T(8,128)(2,1)} %get-tuple-element.16.enc_ref, bf16[4096,256]{1,0:T(8,128)(2,1)} %kw_ref.3, bf16[4096,256]{1,0:T(8,128)(2,1)} %vw_ref.3, ...), custom_call_target="tpu_custom_call" | custom-call | tf_op jit(solution)/shard_map/reduce_all/pallas_call | solution.py:725
  167.6 1.7 copy.40
  169.3 1.7 copy.41
  171.0 1.7 copy.42
  172.6 1.7 copy.43
  (32 shorter events, 1.0 us)
Async XLA Ops:
  1.4 1.6 copy-start.5
  3.0 1.6 copy-start.6
  4.6 0.9 copy-start.9
  5.6 0.9 copy-start.10
  6.5 0.9 copy-start.11
  59.6 2.0 %copy-start = (bf16[16,512,256]{2,1,0:T(8,128)(2,1)}, bf16[16,512,256]{2,1,0:T(8,128)(2,1)S(1)}, u32[]{:S(2)}) copy-start(bf16[16,512,256]{2,1,0:T(8,128)(2,1)S(1)} %get-tuple-element.12.q_all) | copy-start | bytes 12582916
  61.6 2.0 %copy-start.3 = (bf16[16,512,256]{2,1,0:T(8,128)(2,1)}, bf16[16,512,256]{2,1,0:T(8,128)(2,1)S(1)}, u32[]{:S(2)}) copy-start(bf16[16,512,256]{2,1,0:T(8,128)(2,1)S(1)} %get-tuple-element.13.g_all) | copy-start | bytes 12582916
  66.2 2.2 %copy-start.1 = (bf16[16,512,256]{2,1,0:T(8,128)(2,1)S(1)}, bf16[16,512,256]{2,1,0:T(8,128)(2,1)}, u32[]{:S(2)}) copy-start(bf16[16,512,256]{2,1,0:T(8,128)(2,1)} %copy-done) | copy-start | bytes 12582916
  68.4 2.2 %copy-start.4 = (bf16[16,512,256]{2,1,0:T(8,128)(2,1)S(1)}, bf16[16,512,256]{2,1,0:T(8,128)(2,1)}, u32[]{:S(2)}) copy-start(bf16[16,512,256]{2,1,0:T(8,128)(2,1)} %copy-done.3) | copy-start | bytes 12582916
  70.5 24.6 %copy-start.2 = (bf16[16,512,256]{2,1,0:T(8,128)(2,1)S(1)}, bf16[16,512,256]{2,1,0:T(8,128)(2,1)}, u32[]{:S(2)}) copy-start(bf16[16,512,256]{2,1,0:T(8,128)(2,1)} %copy-done) | copy-start | bytes 12582916
  110.6 2.0 %copy-start.7 = (bf16[16,512,256]{2,1,0:T(8,128)(2,1)}, bf16[16,512,256]{2,1,0:T(8,128)(2,1)S(1)}, u32[]{:S(2)}) copy-start(bf16[16,512,256]{2,1,0:T(8,128)(2,1)S(1)} %get-tuple-element.17.dq_ref) | copy-start | bytes 12582916
  112.6 0.8 copy-start.8

commit v2 on v0

v2 whole, which is shorter than its diff:
```python
import math

import jax
import jax.numpy as jnp
from jax import lax
from jax.experimental import pallas as pl
from jax.experimental.pallas import tpu as pltpu
from jax.sharding import PartitionSpec as P

HD = 128
SPAN = 64
NL = 128
K = 2
NB_DEV = 4
HEADS = 2
DP = 16
MP = 16
ZN = 8
SIDE = 4
SHARD = 256
ROWS = 512
HALF = 256
CHUNK = 128
PAIR = 2 * SPAN
MESH = pl.DeviceIdType.MESH
SCALE = 1.0 / math.sqrt(HD)
OFFSETS = (0, -1, 1, 2)
SPAN_MASK = 7
RING = (4, 3, -3, 2, -2, 1, -1, 0)
NT = (((1,), (1,)), ((), ()))
NN = (((1,), (0,)), ((), ()))
TN = (((0,), (0,)), ((), ()))
BF16, F32, I32 = jnp.bfloat16, jnp.float32, jnp.int32


def dot(a, b, dims):
    return lax.dot_general(a, b, dims, preferred_element_type=F32)


def wrap(value, size):
    return lax.rem(value + size, size)


class Place:
    def __init__(self):
        self.dp = lax.axis_index("dp")
        self.mp = lax.axis_index("mp")
        self.z, self.core = lax.div(self.dp, 2), lax.rem(self.dp, 2)
        self.x, self.y = lax.div(self.mp, SIDE), lax.rem(self.mp, SIDE)
        self.sibling = self.z * 2 + 1 - self.core

    def along_z(self, step, other_core=False):
        core = 1 - self.core if other_core else self.core
        return wrap(self.z + step, ZN) * 2 + core

    def in_plane(self, path, first, second):
        along_x, along_y = (first, second) if path == 0 else (second, first)
        return wrap(self.x + along_x, SIDE) * SIDE + wrap(self.y + along_y, SIDE)

    def plane_neighbour(self, path, axis, way):
        step = 1 if way == 0 else -1
        return self.in_plane(path, step, 0) if axis == 0 else self.in_plane(path, 0, step)

    def z_device(self, way):
        return (self.along_z(1 if way == 0 else -1), self.mp)

    def greet(self):
        barrier = pltpu.get_barrier_semaphore()
        others = [(wrap(self.dp + k, DP), self.mp) for k in range(1, DP)]
        others += [(self.dp, self.plane_neighbour(0, axis, way)) for axis in (0, 1) for way in (0, 1)]
        for device in others:
            pl.semaphore_signal(barrier, inc=1, device_id=device, device_id_type=MESH)
        pl.semaphore_wait(barrier, len(others))


def send(src, dst, send_sem, recv_sem, device):
    pltpu.make_async_remote_copy(
        src_ref=src,
        dst_ref=dst,
        send_sem=send_sem,
        recv_sem=recv_sem,
        device_id=device,
        device_id_type=MESH,
    ).start()


def landed(ref, sem):
    pltpu.make_async_copy(ref, ref, sem).wait()


def kernel(
    ids_ref, q_ref, g_ref, e_ref, kw_ref, vw_ref,
    dq_out, eg_out, kg_out, vg_out,
    q_all, g_all, ids_all, tab, enc, w, acc, kv, kt, q_sel, g_sel, score_sv, pgrad_sv, st_own, st_all,
    dqs, dqr, bg, csb, crb, zsb, zrb, xs1, xr1, xs2, xr2, group, ys1, yr1, ys2, yr2,
    local_sem, sent, zr, cr, ir, icr, p1r, p1f, p2r, p2f, sr, scr, dqrs, wcr, wzr, x1r, x2r, y1r, y2r,
):
    at = Place()
    here = (at.sibling, at.mp)
    srcs, alls = (q_ref, g_ref), (q_all, g_all)
    own_cols = [slice(h * HD, (h + 1) * HD) for h in range(HEADS)]

    ids_all[at.dp] = ids_ref[...]
    at.greet()

    def z_send(way, step, kind, h):
        origin = at.along_z(1 - step if way == 0 else step - 1)
        dst = alls[kind].at[h, origin]
        src = srcs[kind].at[:, own_cols[h]] if step == 1 else dst
        send(src, dst, sent.at[h], zr.at[h, kind, way, step - 1], at.z_device(way))

    def core_send(which, kind, h, origin):
        dst = alls[kind].at[h, origin]
        src = srcs[kind].at[:, own_cols[h]] if which == 0 else dst
        distance = which if which < 5 else which - 4
        send(src, dst, sent.at[2 + h], cr.at[h, max(distance - 2, 0)], here)

    def carries(way, step, kind):
        return step < 4 or (step == 4 and way == kind)

    def z_arrive(step, h):
        for kind in (0, 1):
            for way in (0, 1):
                if not carries(way, step, kind):
                    continue
                origin = at.along_z(-step if way == 0 else step)
                landed(alls[kind].at[h, origin], zr.at[h, kind, way, step - 1])
                if carries(way, step + 1, kind):
                    z_send(way, step + 1, kind, h)
                core_send(way * 4 + step, kind, h, origin)

    def z_start(h):
        for kind in (0, 1):
            for way in (0, 1):
                z_send(way, 1, kind, h)
        for kind in (0, 1):
            core_send(0, kind, h, at.dp)

    def core_arrived(h, near):
        landed(q_all.at[h, pl.ds(0, (10, 4, 2)[near])], cr.at[h, near])

    def ids_send(way, step):
        block = ids_all.at[at.along_z(1 - step if way == 0 else step - 1)]
        send(block, block, sent.at[4], ir.at[way, step - 1], at.z_device(way))

    def ids_core(origin):
        block = ids_all.at[origin]
        send(block, block, sent.at[5], icr.at[0], here)

    def ids_arrive(step):
        for way in (0, 1):
            if step == 4 and way == 1:
                continue
            origin = at.along_z(-step if way == 0 else step)
            landed(ids_all.at[origin], ir.at[way, step - 1])
            if step < 3 or (step == 3 and way == 0):
                ids_send(way, step + 1)
            ids_core(origin)

    def lane_sum(value):
        for hop in (64, 32, 16, 8, 4, 2, 1):
            value = value + pltpu.roll(value, hop, 1)
        return value

    def make_tables():
        landed(ids_all.at[pl.ds(0, ZN)], icr.at[0])
        ids = ids_all[:, 0, :]
        slot = lax.broadcasted_iota(I32, (DP, 128), 1)
        owners = jnp.right_shift(ids, 2)
        ranks = jnp.zeros((DP, 128), I32)
        for back in range(1, DP):
            same = (pltpu.roll(owners, back, 1) == owners) & (slot >= back)
            ranks = ranks + jnp.where(same, 1, 0)
        places = owners * 2 + ranks
        even = jnp.bitwise_and(slot, 1) == 0
        partner = jnp.where(even, pltpu.roll(places, 127, 1), pltpu.roll(places, 1, 1))
        code = jnp.right_shift(slot, 1) + 8 * jnp.bitwise_and(ids, 3) + 32 * partner + 1024
        for rank in (0, 1):
            mine = (owners == at.dp) & (ranks == rank) & (slot < DP)
            tab[rank] = lane_sum(jnp.where(mine, code, 0))
        tab[2] = jnp.where(slot < SPAN, tab[0], tab[1])
        tab[3] = places
        own = tab[3, pl.ds(at.dp, 1), :]
        diagonal = slot == lax.broadcasted_iota(I32, (DP, 128), 0)
        tab[3] = lane_sum(jnp.where(diagonal, own, 0))

    def rows_of(path):
        return pl.ds(path * HALF, HALF)

    def part_of(path, way):
        return pl.ds(path * HALF + way * CHUNK, CHUNK)

    def p2_first(path, k):
        origin = at.in_plane(path, OFFSETS[k], 0)
        dst = enc.at[origin, rows_of(path)]
        src = e_ref.at[rows_of(path)] if k == 0 else dst
        for way in (0, 1):
            device = (at.dp, at.plane_neighbour(path, 1, way))
            send(src, dst, sent.at[7], p2r.at[path, k, way], device)

    def p1_first(path):
        for way in (0, 1):
            device = (at.dp, at.plane_neighbour(path, 0, way))
            send(
                e_ref.at[rows_of(path)], enc.at[at.mp, rows_of(path)],
                sent.at[6], p1r.at[path, way], device,
            )

    def p1_arrive(path, way):
        origin = at.in_plane(path, -1 if way == 0 else 1, 0)
        landed(enc.at[origin, rows_of(path)], p1r.at[path, way])
        part = enc.at[origin, part_of(path, way)]
        device = (at.dp, at.plane_neighbour(path, 0, way))
        send(part, part, sent.at[6], p1f.at[path], device)
        p2_first(path, 1 + way)

    def p1_far(path):
        landed(enc.at[at.in_plane(path, 2, 0), rows_of(path)], p1f.at[path])
        p2_first(path, 3)

    def p2_arrive(path, k):
        for way in (0, 1):
            origin = at.in_plane(path, OFFSETS[k], -1 if way == 0 else 1)
            landed(enc.at[origin, rows_of(path)], p2r.at[path, k, way])
            part = enc.at[origin, part_of(path, way)]
            device = (at.dp, at.plane_neighbour(path, 1, way))
            send(part, part, sent.at[7], p2f.at[0], device)

    def p2_far():
        landed(enc.at[pl.ds(0, SIDE)], p2f.at[0])

    def project(h):
        def one(j, total):
            for k in range(SIDE):
                rows = pl.ds(pl.multiple_of((j * SIDE + k) * SHARD, SHARD), SHARD)
                part = dot(enc[j * SIDE + k], w[h, rows, :], NN)
                total = part if k == 0 else total + part
            acc[...] += total
            return total

        acc[...] = jnp.zeros_like(acc)
        lax.fori_loop(0, SIDE, lambda j, c: (one(j, None), c)[1], 0)
        kv[h] = acc[...].astype(BF16)
        kt[h] = jnp.transpose(kv[h, :, :HD])

    low = lax.broadcasted_iota(I32, (1, PAIR), 1) < SPAN

    def chosen(ref, h, i):
        picked = []
        for rank in (0, 1):
            span = jnp.bitwise_and(tab[rank, pl.ds(i, 1), :], SPAN_MASK)
            total = None
            for s in range(ROWS // SPAN):
                factor = jnp.where(span == s, 1.0, 0.0).astype(BF16)
                term = ref[h, i, pl.ds(s * SPAN, SPAN), :] * factor
                total = term if total is None else total + term
            picked.append(total)
        return jnp.concatenate(picked, axis=0)

    def lane_codes(chip):
        return jnp.concatenate([tab[2, pl.ds(chip * 2 + core, 1), :] for core in (0, 1)], axis=1)

    def blocks_of(codes):
        return jnp.bitwise_and(jnp.right_shift(codes, 3), 3)

    def chip_stats(h, chip):
        block = blocks_of(lane_codes(chip))
        for ref, sel in ((q_all, q_sel), (g_all, g_sel)):
            for core in (0, 1):
                sel[h, chip, pl.ds(core * PAIR, PAIR), :] = chosen(ref, h, chip * 2 + core)
        qh, gh = q_sel[h, chip], g_sel[h, chip]
        scores = pgrad = None
        for b in range(NB_DEV):
            rows = pl.ds(b * NL, NL)
            s = dot(kv[h, rows, :HD], qh, NT)
            p = dot(kv[h, rows, HD:], gh, NT)
            scores = s if b == 0 else jnp.where(block == b, s, scores)
            pgrad = p if b == 0 else jnp.where(block == b, p, pgrad)
        scores = scores * SCALE
        top = jnp.max(scores, axis=0, keepdims=True)
        e = jnp.exp(scores - top)
        total = jnp.sum(e, axis=0, keepdims=True)
        lse = top + jnp.log(total)
        delta = jnp.sum(e * pgrad, axis=0, keepdims=True) / total
        for core in (0, 1):
            lanes = slice(core * PAIR, (core + 1) * PAIR)
            st_own[h, pl.ds(chip * 4 + core * 2, 1), :] = lse[:, lanes]
            st_own[h, pl.ds(chip * 4 + core * 2 + 1, 1), :] = delta[:, lanes]
        score_sv[h, chip] = scores
        pgrad_sv[h, chip] = pgrad

    def stats(h, near):
        first, step, count = ((6, 1, 5), (3, 2, 2), (4, 1, 1))[near]

        def one(t, carry):
            chip_stats(h, lax.rem(at.z + first + step * t, ZN))
            return carry

        lax.fori_loop(0, count, one, 0)

    def stats_send(h):
        for k in (4, 3, 5, 2, 6, 1, 7):
            device = (at.along_z(k), at.mp)
            send(st_own.at[h], st_all.at[h, at.dp], sent.at[8 + h], sr.at[h, at.z], device)
        send(st_own.at[h], st_all.at[h, at.dp], sent.at[10 + h], scr.at[h], here)

    def stats_forward(h):
        for k in (1, 7, 2, 6, 3, 5, 4):
            origin = at.along_z(k)
            landed(st_all.at[h, origin], sr.at[h, wrap(at.z + k, ZN)])
            send(st_all.at[h, origin], st_all.at[h, origin], sent.at[10 + h], scr.at[h], here)

    def stats_arrived(h):
        landed(st_all.at[h, pl.ds(0, ZN)], scr.at[h])
        st_all[h, at.dp] = st_own[h]

    def merged(h, i):
        code = tab[2, pl.ds(i, 1), :]
        partner = jnp.bitwise_and(jnp.right_shift(code, 5), 31)
        owner = jnp.right_shift(partner, 1)
        turned = pltpu.roll(owner, SPAN, 1)
        straight = jnp.zeros((2, PAIR), F32)
        crossed = jnp.zeros((2, PAIR), F32)
        for o in range(DP):
            pair = st_all[h, o, pl.ds(i * 2, 2), :]
            straight = jnp.where(owner == o, pair, straight)
            crossed = jnp.where(turned == o, pair, crossed)
        same = (jnp.bitwise_and(partner, 1) == 0) == low
        there = jnp.where(same, straight, pltpu.roll(crossed, SPAN, 1))
        own = st_own[h, pl.ds(i * 2, 2), :]
        lse_here, lse_there = own[:1], there[:1]
        top = jnp.maximum(lse_here, lse_there)
        lse = top + jnp.log(jnp.exp(lse_here - top) + jnp.exp(lse_there - top))
        delta = jnp.exp(lse_here - lse) * own[1:] + jnp.exp(lse_there - lse) * there[1:]
        return lse, delta

    def chip_grads(h, chip):
        codes = lane_codes(chip)
        block = jnp.where(jnp.right_shift(codes, 10) > 0, blocks_of(codes), NB_DEV)
        parts = [merged(h, chip * 2 + core) for core in (0, 1)]
        lse = jnp.concatenate([p[0] for p in parts], axis=1)
        delta = jnp.concatenate([p[1] for p in parts], axis=1)
        prob = jnp.exp(score_sv[h, chip] - lse)
        score_grad = prob * (pgrad_sv[h, chip] - delta) * SCALE
        zero = jnp.zeros_like(prob)
        prob_by_block = jnp.concatenate(
            [jnp.where(block == b, prob, zero).astype(BF16) for b in range(NB_DEV)], axis=0
        )
        grad_by_block = jnp.concatenate(
            [jnp.where(block == b, score_grad, zero).astype(BF16) for b in range(NB_DEV)], axis=0
        )
        acc[:, :HD] += dot(grad_by_block, q_sel[h, chip], NN)
        acc[:, HD:] += dot(prob_by_block, g_sel[h, chip], NN)
        dq = jnp.transpose(dot(kt[h], grad_by_block, NN)).astype(BF16)
        for core in (0, 1):
            dqs[h, chip * 2 + core] = dq[core * PAIR : (core + 1) * PAIR, :]

    def grads(h):
        acc[...] = jnp.zeros_like(acc)

        def one(chip, carry):
            chip_grads(h, chip)
            return carry

        lax.fori_loop(0, ZN, one, 0)
        dqr[h, at.dp] = dqs[h, at.dp]
        bg[h] = acc[...].astype(BF16)

    def dq_send(h, begin, end):
        def one(k, carry):
            i = wrap(at.dp + k, DP)
            send(dqs.at[h, i], dqr.at[h, at.dp], sent.at[12 + h], dqrs.at[h], (i, at.mp))
            return carry

        lax.fori_loop(begin, end, one, 0)

    def dq_final(h):
        landed(dqr.at[h, pl.ds(0, DP - 1)], dqrs.at[h])

        def one(c, carry):
            places = [tab[3, pl.ds(c * K + k, 1), :] for k in range(K)]
            total = jnp.zeros((SPAN, HD), BF16)
            for m in range(2 * DP):
                hit = (places[0] == m) | (places[1] == m)
                factor = jnp.where(hit, 1.0, 0.0).astype(BF16)
                total = total + dqr[h, m // 2, pl.ds(m % 2 * SPAN, SPAN), :] * factor
            dq_out[pl.ds(pl.multiple_of(c * SPAN, SPAN), SPAN), own_cols[h]] = total
            return carry

        lax.fori_loop(0, ROWS // SPAN, one, 0)

    def weight_sibling(h, begin, end):
        def one(which, carry):
            near = lax.div(which + 1, 2)
            sign = 2 * lax.rem(which, 2) - 1
            target = wrap(at.z + sign * (4 - near), ZN)
            csb[h, target] = dot(enc[target * 2 + 1 - at.core], bg[h], TN).astype(BF16)
            send(csb.at[h, target], crb.at[h, target], sent.at[14 + h], wcr.at[h, near], here)
            return carry

        lax.fori_loop(begin, end, one, 0)

    def weight_met(h, near):
        landed(crb.at[h, pl.ds(0, 1 if near in (0, 4) else 2)], wcr.at[h, near])

    def weight_term(h, which):
        target = wrap(at.z + RING[which], ZN)
        return dot(enc[target * 2 + at.core], bg[h], TN) + crb[h, target].astype(F32)

    def z_region(step, way):
        return pl.ds(way * CHUNK, CHUNK) if step == 1 else pl.ds(0, SHARD)

    def weight_put(h, way, step, value):
        region = z_region(step, way)
        zsb[h, way, step - 1, region, :] = value.astype(BF16)
        send(
            zsb.at[h, way, step - 1, region], zrb.at[h, way, step - 1, region],
            sent.at[16 + h], wzr.at[h, way, step - 1], at.z_device(way),
        )

    def weight_step(h, step):
        if step == 1:
            weight_met(h, 0)
            value = weight_term(h, 0)
            for way in (0, 1):
                weight_put(h, way, 1, value[way * CHUNK : (way + 1) * CHUNK, :])
            return
        weight_met(h, step - 1)
        for way in (0, 1):
            which = 2 * step - 3 + way
            value = weight_term(h, which)
            region = z_region(step - 1, way)
            landed(zrb.at[h, way, step - 2, region], wzr.at[h, way, step - 2])
            came = zrb[h, way, step - 2, region, :].astype(F32)
            if step == 2:
                pieces = [value[:CHUNK, :], value[CHUNK:, :]]
                pieces[way] = pieces[way] + came
                value = jnp.concatenate(pieces, axis=0)
            else:
                value = value + came
            weight_put(h, way, step, value)

    def weight_final(h):
        weight_met(h, 4)
        value = weight_term(h, 7)
        for way in (0, 1):
            landed(zrb.at[h, way, 3], wzr.at[h, way, 3])
            value = value + zrb[h, way, 3].astype(F32)
        kg_out[:, own_cols[h]] = value[:, :HD]
        vg_out[:, own_cols[h]] = value[:, HD:]

    def width_part(path, offset, j):
        if path == 0:
            index = wrap(at.x + offset, SIDE) * SIDE + j
        else:
            index = j * SIDE + wrap(at.y + offset, SIDE)
        cols = pl.ds(pl.multiple_of(index * SHARD, SHARD), SHARD)
        return sum(dot(bg[h, rows_of(path), :], w[h, cols, :], NT) for h in range(HEADS))

    def width_far(path):
        def one(j, carry):
            value = width_part(path, 2, j).astype(BF16)
            for way in (0, 1):
                xs1[path, way, j] = value[way * CHUNK : (way + 1) * CHUNK, :]
            return carry

        lax.fori_loop(0, SIDE, one, 0)
        for way in (0, 1):
            device = (at.dp, at.plane_neighbour(path, 0, way))
            send(xs1.at[path, way], xr1.at[path, way], sent.at[18], x1r.at[path, way], device)

    def width_near(path, way):
        landed(xr1.at[path, way], x1r.at[path, way])

        def one(j, carry):
            value = width_part(path, 1 if way == 0 else -1, j)
            came = xr1[path, way, j].astype(F32)
            for part in (0, 1):
                piece = value[part * CHUNK : (part + 1) * CHUNK, :]
                piece = piece + came if part == way else piece
                xs2[path, way, j, pl.ds(part * CHUNK, CHUNK), :] = piece.astype(BF16)
            return carry

        lax.fori_loop(0, SIDE, one, 0)
        device = (at.dp, at.plane_neighbour(path, 0, way))
        send(xs2.at[path, way], xr2.at[path, way], sent.at[19], x2r.at[path], device)

    def second(path):
        return at.y if path == 0 else at.x

    def width_own(path):
        landed(xr2.at[path], x2r.at[path])

        def one(j, carry):
            value = width_part(path, 0, j)
            for way in (0, 1):
                value = value + xr2[path, way, j].astype(F32)
            group[path, j] = value
            return carry

        lax.fori_loop(0, SIDE, one, 0)
        far = wrap(second(path) + 2, SIDE)
        for way in (0, 1):
            ys1[path, way] = group[path, far, pl.ds(way * CHUNK, CHUNK), :].astype(BF16)
            device = (at.dp, at.plane_neighbour(path, 1, way))
            send(ys1.at[path, way], yr1.at[path, way], sent.at[20], y1r.at[path, way], device)

    def width_second(path):
        for way in (0, 1):
            landed(yr1.at[path, way], y1r.at[path, way])
            near = wrap(second(path) + (1 if way == 0 else -1), SIDE)
            for part in (0, 1):
                piece = group[path, near, pl.ds(part * CHUNK, CHUNK), :]
                if part == way:
                    piece = piece + yr1[path, way].astype(F32)
                ys2[path, way, pl.ds(part * CHUNK, CHUNK), :] = piece.astype(BF16)
            device = (at.dp, at.plane_neighbour(path, 1, way))
            send(ys2.at[path, way], yr2.at[path, way], sent.at[21], y2r.at[path], device)

    def width_final(path):
        value = group[path, second(path)]
        landed(yr2.at[path], y2r.at[path])
        for way in (0, 1):
            value = value + yr2[path, way].astype(F32)
        eg_out[pl.ds(path * HALF, HALF), :] = value.astype(BF16)

    def finish():
        for h in range(HEADS):
            landed(q_all.at[h, pl.ds(0, 14)], sent.at[h])
            landed(q_all.at[h], sent.at[2 + h])
            landed(st_all.at[h, pl.ds(0, ZN - 1)], sent.at[8 + h])
            landed(st_all.at[h, pl.ds(0, ZN)], sent.at[10 + h])
            landed(dqr.at[h, pl.ds(0, DP - 1)], sent.at[12 + h])
            landed(crb.at[h], sent.at[14 + h])
            landed(crb.at[h, pl.ds(0, 7)], sent.at[16 + h])
        landed(ids_all.at[pl.ds(0, 7)], sent.at[4])
        landed(ids_all.at[pl.ds(0, ZN)], sent.at[5])
        landed(enc.at[pl.ds(0, 3)], sent.at[6])
        landed(enc.at[pl.ds(0, 12)], sent.at[7])
        for n, ref in enumerate((xr1, xr2, yr1, yr2)):
            landed(ref, sent.at[18 + n])

    for way in (0, 1):
        ids_send(way, 1)
    z_start(0)
    ids_core(at.dp)
    for path in (0, 1):
        p1_first(path)
    for path in (0, 1):
        p2_first(path, 0)
    pltpu.make_async_copy(e_ref, enc.at[at.mp], local_sem.at[0]).start()
    for h in range(HEADS):
        cols = own_cols[h]
        pltpu.make_async_copy(q_ref.at[:, cols], q_all.at[h, at.dp], local_sem.at[1]).start()
        pltpu.make_async_copy(g_ref.at[:, cols], g_all.at[h, at.dp], local_sem.at[1]).start()
        pltpu.make_async_copy(kw_ref.at[:, cols], w.at[h, :, pl.ds(0, HD)], local_sem.at[2]).start()
        pltpu.make_async_copy(vw_ref.at[:, cols], w.at[h, :, pl.ds(HD, HD)], local_sem.at[2]).start()

    for way in (0, 1):
        for path in (0, 1):
            p1_arrive(path, way)
    ids_arrive(1)
    for path in (0, 1):
        p2_arrive(path, 0)
    z_arrive(1, 0)
    for path in (0, 1):
        p1_far(path)
    ids_arrive(2)
    for path in (0, 1):
        p2_arrive(path, 1)
    z_arrive(2, 0)
    z_start(1)
    for path in (0, 1):
        p2_arrive(path, 2)
    ids_arrive(3)
    for path in (0, 1):
        p2_arrive(path, 3)
    z_arrive(3, 0)
    ids_arrive(4)
    p2_far()
    landed(enc.at[0], local_sem.at[0])
    landed(q_all.at[0, pl.ds(0, 4)], local_sem.at[1])
    landed(w, local_sem.at[2])
    make_tables()
    z_arrive(1, 1)
    project(0)
    core_arrived(0, 0)
    stats(0, 0)
    z_arrive(4, 0)
    z_arrive(2, 1)
    core_arrived(0, 1)
    stats(0, 1)
    core_arrived(0, 2)
    stats(0, 2)
    stats_send(0)
    project(1)
    z_arrive(3, 1)
    stats_forward(0)
    core_arrived(1, 0)
    stats(1, 0)
    stats_arrived(0)
    grads(0)
    z_arrive(4, 1)
    core_arrived(1, 1)
    stats(1, 1)
    core_arrived(1, 2)
    stats(1, 2)
    stats_send(1)
    dq_send(0, 1, DP)
    weight_sibling(0, 0, 3)
    weight_step(0, 1)
    stats_forward(1)
    weight_sibling(0, 3, 8)
    weight_step(0, 2)
    stats_arrived(1)
    grads(1)
    weight_sibling(1, 0, 3)
    weight_step(1, 1)
    dq_send(1, 1, DP)
    weight_step(0, 3)
    for path in (0, 1):
        width_far(path)
    weight_sibling(1, 3, 8)
    weight_step(1, 2)
    weight_step(0, 4)
    for path in (0, 1):
        width_near(path, 0)
    weight_step(1, 3)
    for path in (0, 1):
        width_near(path, 1)
    weight_final(0)
    for path in (0, 1):
        width_own(path)
    weight_step(1, 4)
    dq_final(0)
    for path in (0, 1):
        width_second(path)
    for path in (0, 1):
        width_final(path)
    dq_final(1)
    weight_final(1)
    finish()


def publish_kernel(a, b, c, d, a_out, b_out, c_out, d_out):
    for src, dst in ((a, a_out), (b, b_out), (c, c_out), (d, d_out)):
        dst[...] = src[...]


def body(queries, grad_attn, encoded, key_weight, value_weight, nbr_ids):
    hbm = pl.BlockSpec(memory_space=pltpu.HBM)
    vmem = pl.BlockSpec(memory_space=pltpu.VMEM)
    dma = pltpu.SemaphoreType.DMA
    shapes = (
        jax.ShapeDtypeStruct((ROWS, SHARD), BF16),
        jax.ShapeDtypeStruct((ROWS, SHARD), BF16),
        jax.ShapeDtypeStruct((SHARD, SHARD), F32),
        jax.ShapeDtypeStruct((SHARD, SHARD), F32),
    )
    ids = jnp.pad(nbr_ids.reshape(1, DP), ((0, 7), (0, 128 - DP)))
    results = pl.pallas_call(
        kernel,
        out_shape=shapes,
        in_specs=[vmem] + [hbm] * 5,
        out_specs=(vmem, vmem, vmem, vmem),
        scratch_shapes=[
            pltpu.VMEM((HEADS, DP, ROWS, HD), BF16),
            pltpu.VMEM((HEADS, DP, ROWS, HD), BF16),
            pltpu.VMEM((DP, 8, 128), I32),
            pltpu.VMEM((4, DP, 128), I32),
            pltpu.VMEM((MP, ROWS, SHARD), BF16),
            pltpu.VMEM((HEADS, MP * SHARD, 2 * HD), BF16),
            pltpu.VMEM((ROWS, 2 * HD), F32),
            pltpu.VMEM((HEADS, ROWS, 2 * HD), BF16),
            pltpu.VMEM((HEADS, HD, ROWS), BF16),
            pltpu.VMEM((HEADS, ZN, 2 * PAIR, HD), BF16),
            pltpu.VMEM((HEADS, ZN, 2 * PAIR, HD), BF16),
            pltpu.VMEM((HEADS, ZN, NL, 2 * PAIR), F32),
            pltpu.VMEM((HEADS, ZN, NL, 2 * PAIR), F32),
            pltpu.VMEM((HEADS, DP * 2, PAIR), F32),
            pltpu.VMEM((HEADS, DP, DP * 2, PAIR), F32),
            pltpu.VMEM((HEADS, DP, PAIR, HD), BF16),
            pltpu.VMEM((HEADS, DP, PAIR, HD), BF16),
            pltpu.VMEM((HEADS, ROWS, 2 * HD), BF16),
            pltpu.VMEM((HEADS, ZN, SHARD, 2 * HD), BF16),
            pltpu.VMEM((HEADS, ZN, SHARD, 2 * HD), BF16),
            pltpu.VMEM((HEADS, 2, 4, SHARD, 2 * HD), BF16),
            pltpu.VMEM((HEADS, 2, 4, SHARD, 2 * HD), BF16),
            pltpu.VMEM((2, 2, SIDE, CHUNK, SHARD), BF16),
            pltpu.VMEM((2, 2, SIDE, CHUNK, SHARD), BF16),
            pltpu.VMEM((2, 2, SIDE, HALF, SHARD), BF16),
            pltpu.VMEM((2, 2, SIDE, HALF, SHARD), BF16),
            pltpu.VMEM((2, SIDE, HALF, SHARD), F32),
            pltpu.VMEM((2, 2, CHUNK, SHARD), BF16),
            pltpu.VMEM((2, 2, CHUNK, SHARD), BF16),
            pltpu.VMEM((2, 2, HALF, SHARD), BF16),
            pltpu.VMEM((2, 2, HALF, SHARD), BF16),
            dma((3,)), dma((22,)),
            dma((HEADS, 2, 2, 4)), dma((HEADS, 3)),
            dma((2, 4)), dma((1,)),
            dma((2, 2)), dma((2,)), dma((2, 4, 2)), dma((1,)),
            dma((HEADS, ZN)), dma((HEADS,)), dma((HEADS,)),
            dma((HEADS, 5)), dma((HEADS, 2, 4)),
            dma((2, 2)), dma((2,)), dma((2, 2)), dma((2,)),
        ],
        compiler_params=pltpu.CompilerParams(
            collective_id=0, has_side_effects=True, vmem_limit_bytes=60 * 2**20
        ),
        name="retro_backward",
    )(ids, queries, grad_attn, encoded, key_weight, value_weight)
    return pl.pallas_call(
        publish_kernel,
        out_shape=shapes,
        in_specs=[vmem] * 4,
        out_specs=(vmem,) * 4,
        name="publish",
    )(*results)


def solution(mesh):
    return jax.shard_map(
        body,
        mesh=mesh,
        in_specs=(
            P("dp", "mp"),
            P("dp", "mp"),
            P("dp", "mp"),
            P(None, "mp"),
            P(None, "mp"),
            P("dp", None),
        ),
        out_specs=(P("dp", "mp"), P("dp", "mp"), P("dp", "mp"), P("dp", "mp")),
        check_vma=False,
    )
```

time: 511 us -> 145 us (0.28)
  waiting for transfers between devices: 276 us -> 0 us
  Pallas kernels: 0 us -> 142 us
  blocking collectives: 119 us -> 0 us
  matrix products: 43 us -> 0 us
  local copies, waits for them, and re-layouts: 41.6 us -> 1.44 us
  between operations: 13.9 us -> 0.64 us
  other arithmetic: 8.63 us -> 0 us
  starting transfers between devices: 7.64 us -> 0 us
    pallas_call x0 -> x2, Pallas kernels: none -> 142 us  [the longest x1 140 us: body(): pl.pallas_call(kernel, out_shape=shapes, in_specs=[vmem] + [hbm] * 5, out...]
    reduce_scatter x2 -> x0, waiting for transfers between devices: 140 us -> none  [the longest x1 89.6 us: body(): lax.psum_scatter(width_terms, 'mp', scatter_dimension=1, tiled=True)]
    all_to_all x1 -> x0, blocking collectives: 99.2 us -> none  [body(): lax.all_to_all(return_buf.reshape(dp_count, capacity, NL, 2 * head_cols),...]
    all_to_all x1 -> x0, waiting for transfers between devices: 92.9 us -> none  [body(): lax.all_to_all(outgoing, 'dp', split_axis=0, concat_axis=0, tiled=True)]
    dot_general x9 -> x0, matrix products: 43 us -> none  [the longest x1 8.42 us: body(): jnp.einsum('chqk,cqhd->ckhd', score_grad, query_blocks, preferred_element...]
    all_gather x1 -> x0, waiting for transfers between devices: 41.6 us -> none  [body(): whole_enc = lax.all_gather(encoded, 'mp', axis=1, tiled=True)]
    all_gather x1 -> x0, blocking collectives: 20.2 us -> none  [body(): lax.all_gather(nbr_ids, 'dp', axis=0, tiled=True)]
    reshape x8 -> x1, local copies, waits for them, and re-layouts: 16.3 us -> 0.08 us  [body(): ids = jnp.pad(nbr_ids.reshape(1, DP), ((0, 7), (0, 128 - DP)))]
  transfers between devices with their start and end apart: 4 -> 0, of which waited for: 4 -> 0; matrix products, arithmetic and copies ran while one was open for 5% -> 0% of each run, Pallas kernels for 0% -> 0%
where the time goes in v2:
time: 145 us; the launch traced here: 144 us
  Pallas kernels  142 us (98%)
    pallas_call x1, Pallas kernels, body(): pl.pallas_call(kernel, out_shape=shapes, in_specs=[vmem] + [hbm] * 5, out...  140 us

profile of v2, /device:TPU:2, one launch (start us, length us, event | category | flops | bytes accessed | tf_op | source)
XLA Modules:
  0.0 144.4 jit_solution(3501801919335359672)
XLA Ops:
  0.6 0.8 copy.11
  1.4 0.1 reshape.11
  1.5 0.6 pad.4.ids_ref
  2.1 140.1 %retro_backward.1 = (bf16[512,256]{1,0:T(8,128)(2,1)}, bf16[512,256]{1,0:T(8,128)(2,1)}, f32[256,256]{1,0:T(8,128)}, f32[256,256]{1,0:T(8,128)}) custom-call(s32[8,128]{1,0:T(8,128)} %pad.4.ids_ref, bf16[512,256]{1,0:T(8,128)(2,1)} %q_ref.1, bf16[512,256]{1,0:T(8,128)(2,1)} %g_ref.1, bf16[512,256]{1,0:T(8,128)(2,1)} %e_ref.1, bf16[4096,256]{1,0:T(8,128)(2,1)} %kw_ref.1, ...), custom_call_target="tpu_custom_call" | custom-call | tf_op jit(solution)/shard_map/retro_backward/pallas_call | solution.py:661
  142.2 2.2 %publish.1 = (bf16[512,256]{1,0:T(8,128)(2,1)}, bf16[512,256]{1,0:T(8,128)(2,1)}, f32[256,256]{1,0:T(8,128)}, f32[256,256]{1,0:T(8,128)}) custom-call(bf16[512,256]{1,0:T(8,128)(2,1)} %get-tuple-element.8.a, bf16[512,256]{1,0:T(8,128)(2,1)} %get-tuple-element.9.b, f32[256,256]{1,0:T(8,128)} %get-tuple-element.10.c, f32[256,256]{1,0:T(8,128)} %get-tuple-element.11.d), custom_call_target="tpu_custom_call" | custom-call | tf_op jit(solution)/shard_map/publish/pallas_call | solution.py:711

commit v3 on v2

--- a/solution.py
+++ b/solution.py
@@ -91,8 +91,8 @@
 def kernel(
     ids_ref, q_ref, g_ref, e_ref, kw_ref, vw_ref,
     dq_out, eg_out, kg_out, vg_out,
-    q_all, g_all, ids_all, tab, enc, w, acc, kv, kt, q_sel, g_sel, score_sv, pgrad_sv, st_own, st_all,
-    dqs, dqr, bg, csb, crb, zsb, zrb, xs1, xr1, xs2, xr2, group, ys1, yr1, ys2, yr2,
+    q_all, g_all, ids_all, tab, enc, w, kacc, acc, kv, kt, q_sel, g_sel, score_sv, pgrad_sv, st_own, st_all,
+    dqs, dqr, bg, csb, crb, zsb, zrb, xs1, xr1, near, xs2, xr2, group, ys1, yr1, ys2, yr2,
     local_sem, sent, zr, cr, ir, icr, p1r, p1f, p2r, p2f, sr, scr, dqrs, wcr, wzr, x1r, x2r, y1r, y2r,
 ):
     at = Place()
@@ -118,16 +118,15 @@
     def carries(way, step, kind):
         return step < 4 or (step == 4 and way == kind)
 
-    def z_arrive(step, h):
-        for kind in (0, 1):
-            for way in (0, 1):
-                if not carries(way, step, kind):
-                    continue
-                origin = at.along_z(-step if way == 0 else step)
-                landed(alls[kind].at[h, origin], zr.at[h, kind, way, step - 1])
-                if carries(way, step + 1, kind):
-                    z_send(way, step + 1, kind, h)
-                core_send(way * 4 + step, kind, h, origin)
+    def z_arrive(step, h, kind):
+        for way in (0, 1):
+            if not carries(way, step, kind):
+                continue
+            origin = at.along_z(-step if way == 0 else step)
+            landed(alls[kind].at[h, origin], zr.at[h, kind, way, step - 1])
+            if carries(way, step + 1, kind):
+                z_send(way, step + 1, kind, h)
+            core_send(way * 4 + step, kind, h, origin)
 
     def z_start(h):
         for kind in (0, 1):
@@ -229,19 +228,35 @@
     def p2_far():
         landed(enc.at[pl.ds(0, SIDE)], p2f.at[0])
 
-    def project(h):
-        def one(j, total):
-            for k in range(SIDE):
-                rows = pl.ds(pl.multiple_of((j * SIDE + k) * SHARD, SHARD), SHARD)
-                part = dot(enc[j * SIDE + k], w[h, rows, :], NN)
-                total = part if k == 0 else total + part
-            acc[...] += total
-            return total
-
-        acc[...] = jnp.zeros_like(acc)
-        lax.fori_loop(0, SIDE, lambda j, c: (one(j, None), c)[1], 0)
-        kv[h] = acc[...].astype(BF16)
-        kt[h] = jnp.transpose(kv[h, :, :HD])
+    def project_near(path, k):
+        def one(h, carry):
+            total = None
+            for second in (0, -1, 1):
+                origin = at.in_plane(path, OFFSETS[k], second)
+                rows = pl.ds(pl.multiple_of(origin * SHARD, SHARD), SHARD)
+                part = dot(enc[origin, rows_of(path), :], w[h, rows, :], NN)
+                total = part if total is None else total + part
+            if k == 0:
+                kacc[h, rows_of(path), :] = total
+            else:
+                kacc[h, rows_of(path), :] += total
+            return carry
+
+        lax.fori_loop(0, HEADS, one, 0)
+
+    def project_far():
+        def one(h, carry):
+            for path in (0, 1):
+                total = kacc[h, rows_of(path), :]
+                for k in range(SIDE):
+                    origin = at.in_plane(path, OFFSETS[k], 2)
+                    rows = pl.ds(pl.multiple_of(origin * SHARD, SHARD), SHARD)
+                    total = total + dot(enc[origin, rows_of(path), :], w[h, rows, :], NN)
+                kv[h, rows_of(path), :] = total.astype(BF16)
+            kt[h] = jnp.transpose(kv[h, :, :HD])
+            return carry
+
+        lax.fori_loop(0, HEADS, one, 0)
 
     low = lax.broadcasted_iota(I32, (1, PAIR), 1) < SPAN
 
@@ -265,9 +280,6 @@
 
     def chip_stats(h, chip):
         block = blocks_of(lane_codes(chip))
-        for ref, sel in ((q_all, q_sel), (g_all, g_sel)):
-            for core in (0, 1):
-                sel[h, chip, pl.ds(core * PAIR, PAIR), :] = chosen(ref, h, chip * 2 + core)
         qh, gh = q_sel[h, chip], g_sel[h, chip]
         scores = pgrad = None
         for b in range(NB_DEV):
@@ -289,14 +301,26 @@
         score_sv[h, chip] = scores
         pgrad_sv[h, chip] = pgrad
 
-    def stats(h, near):
-        first, step, count = ((6, 1, 5), (3, 2, 2), (4, 1, 1))[near]
+    def chips(h, distance, work):
+        first, step, count = ((6, 1, 5), (3, 2, 2), (4, 1, 1))[distance]
 
         def one(t, carry):
-            chip_stats(h, lax.rem(at.z + first + step * t, ZN))
+            work(h, lax.rem(at.z + first + step * t, ZN))
             return carry
 
         lax.fori_loop(0, count, one, 0)
+
+    def chip_select(h, chip):
+        for ref, sel in ((q_all, q_sel), (g_all, g_sel)):
+            for core in (0, 1):
+                sel[h, chip, pl.ds(core * PAIR, PAIR), :] = chosen(ref, h, chip * 2 + core)
+
+    def select(h, distance):
+        core_arrived(h, distance)
+        chips(h, distance, chip_select)
+
+    def stats(h, distance):
+        chips(h, distance, chip_stats)
 
     def stats_send(h):
         for k in (4, 3, 5, 2, 6, 1, 7):
@@ -355,24 +379,35 @@
         for core in (0, 1):
             dqs[h, chip * 2 + core] = dq[core * PAIR : (core + 1) * PAIR, :]
 
-    def grads(h):
+    def grads_begin(h):
         acc[...] = jnp.zeros_like(acc)
 
-        def one(chip, carry):
+    def grads_part(h, begin, end, sends):
+        def one(t, carry):
+            chip = lax.rem(at.z + 1 + t, ZN)
             chip_grads(h, chip)
+            if sends:
+                for core in (0, 1):
+                    dq_copy(h, chip * 2 + core)
             return carry
 
-        lax.fori_loop(0, ZN, one, 0)
+        lax.fori_loop(begin, end, one, 0)
+
+    def grads_end(h):
+        chip_grads(h, at.z)
         dqr[h, at.dp] = dqs[h, at.dp]
         bg[h] = acc[...].astype(BF16)
 
-    def dq_send(h, begin, end):
-        def one(k, carry):
-            i = wrap(at.dp + k, DP)
-            send(dqs.at[h, i], dqr.at[h, at.dp], sent.at[12 + h], dqrs.at[h], (i, at.mp))
-            return carry
-
-        lax.fori_loop(begin, end, one, 0)
+    def dq_copy(h, i):
+        send(dqs.at[h, i], dqr.at[h, at.dp], sent.at[12 + h], dqrs.at[h], (i, at.mp))
+
+    def dq_send(h, offsets):
+        for offset in offsets:
+            for other_core in (False, True):
+                if offset == 0 and not other_core:
+                    continue
+                i = at.along_z(offset, other_core)
+                dq_copy(h, i)
 
     def dq_final(h):
         landed(dqr.at[h, pl.ds(0, DP - 1)], dqrs.at[h])
@@ -469,33 +504,53 @@
             device = (at.dp, at.plane_neighbour(path, 0, way))
             send(xs1.at[path, way], xr1.at[path, way], sent.at[18], x1r.at[path, way], device)
 
-    def width_near(path, way):
+    def width_near(path):
+        for way in (0, 1):
+            def one(j, carry):
+                value = width_part(path, 1 if way == 0 else -1, j)
+                pieces = [value[:CHUNK, :], value[CHUNK:, :]]
+                xs2[path, way, 1 - way, j] = pieces[1 - way].astype(BF16)
+                near[path, way, j] = pieces[way]
+                return carry
+
+            lax.fori_loop(0, SIDE, one, 0)
+            near_send(path, way, 1 - way)
+
+    def near_send(path, way, part):
+        device = (at.dp, at.plane_neighbour(path, 0, way))
+        send(xs2.at[path, way, part], xr2.at[path, way, part], sent.at[19], x2r.at[path], device)
+
+    def width_met(path, way):
         landed(xr1.at[path, way], x1r.at[path, way])
-
-        def one(j, carry):
-            value = width_part(path, 1 if way == 0 else -1, j)
-            came = xr1[path, way, j].astype(F32)
-            for part in (0, 1):
-                piece = value[part * CHUNK : (part + 1) * CHUNK, :]
-                piece = piece + came if part == way else piece
-                xs2[path, way, j, pl.ds(part * CHUNK, CHUNK), :] = piece.astype(BF16)
-            return carry
-
-        lax.fori_loop(0, SIDE, one, 0)
-        device = (at.dp, at.plane_neighbour(path, 0, way))
-        send(xs2.at[path, way], xr2.at[path, way], sent.at[19], x2r.at[path], device)
+        for j in range(SIDE):
+            xs2[path, way, way, j] = (near[path, way, j] + xr1[path, way, j].astype(F32)).astype(BF16)
+        near_send(path, way, way)
 
     def second(path):
         return at.y if path == 0 else at.x
 
     def width_own(path):
+        def one(j, carry):
+            group[path, j] = width_part(path, 0, j)
+            return carry
+
+        lax.fori_loop(0, SIDE, one, 0)
+
+    def second_send(path, way, part):
+        device = (at.dp, at.plane_neighbour(path, 1, way))
+        send(ys2.at[path, way, part], yr2.at[path, way, part], sent.at[21], y2r.at[path], device)
+
+    def second_near(path, way):
+        return wrap(second(path) + (1 if way == 0 else -1), SIDE)
+
+    def width_turn(path):
         landed(xr2.at[path], x2r.at[path])
 
         def one(j, carry):
-            value = width_part(path, 0, j)
-            for way in (0, 1):
-                value = value + xr2[path, way, j].astype(F32)
-            group[path, j] = value
+            for part in (0, 1):
+                rows = pl.ds(part * CHUNK, CHUNK)
+                came = xr2[path, 0, part, j].astype(F32) + xr2[path, 1, part, j].astype(F32)
+                group[path, j, rows, :] += came
             return carry
 
         lax.fori_loop(0, SIDE, one, 0)
@@ -504,25 +559,26 @@
             ys1[path, way] = group[path, far, pl.ds(way * CHUNK, CHUNK), :].astype(BF16)
             device = (at.dp, at.plane_neighbour(path, 1, way))
             send(ys1.at[path, way], yr1.at[path, way], sent.at[20], y1r.at[path, way], device)
+        for way in (0, 1):
+            part = 1 - way
+            piece = group[path, second_near(path, way), pl.ds(part * CHUNK, CHUNK), :]
+            ys2[path, way, part] = piece.astype(BF16)
+            second_send(path, way, part)
 
     def width_second(path):
         for way in (0, 1):
             landed(yr1.at[path, way], y1r.at[path, way])
-            near = wrap(second(path) + (1 if way == 0 else -1), SIDE)
-            for part in (0, 1):
-                piece = group[path, near, pl.ds(part * CHUNK, CHUNK), :]
-                if part == way:
-                    piece = piece + yr1[path, way].astype(F32)
-                ys2[path, way, pl.ds(part * CHUNK, CHUNK), :] = piece.astype(BF16)
-            device = (at.dp, at.plane_neighbour(path, 1, way))
-            send(ys2.at[path, way], yr2.at[path, way], sent.at[21], y2r.at[path], device)
+            piece = group[path, second_near(path, way), pl.ds(way * CHUNK, CHUNK), :]
+            ys2[path, way, way] = (piece + yr1[path, way].astype(F32)).astype(BF16)
+            second_send(path, way, way)
 
     def width_final(path):
-        value = group[path, second(path)]
         landed(yr2.at[path], y2r.at[path])
-        for way in (0, 1):
-            value = value + yr2[path, way].astype(F32)
-        eg_out[pl.ds(path * HALF, HALF), :] = value.astype(BF16)
+        for part in (0, 1):
+            value = group[path, second(path), pl.ds(part * CHUNK, CHUNK), :]
+            for way in (0, 1):
+                value = value + yr2[path, way, part].astype(F32)
+            eg_out[pl.ds(path * HALF + part * CHUNK, CHUNK), :] = value.astype(BF16)
 
     def finish():
         for h in range(HEADS):
@@ -559,86 +615,113 @@
     for way in (0, 1):
         for path in (0, 1):
             p1_arrive(path, way)
+    z_arrive(1, 0, 0)
+    z_arrive(1, 0, 1)
+    z_start(1)
+    for path in (0, 1):
+        p2_arrive(path, 0)
     ids_arrive(1)
     for path in (0, 1):
-        p2_arrive(path, 0)
-    z_arrive(1, 0)
-    for path in (0, 1):
         p1_far(path)
-    ids_arrive(2)
-    for path in (0, 1):
-        p2_arrive(path, 1)
-    z_arrive(2, 0)
-    z_start(1)
-    for path in (0, 1):
-        p2_arrive(path, 2)
-    ids_arrive(3)
-    for path in (0, 1):
-        p2_arrive(path, 3)
-    z_arrive(3, 0)
-    ids_arrive(4)
-    p2_far()
+    z_arrive(2, 0, 0)
     landed(enc.at[0], local_sem.at[0])
     landed(q_all.at[0, pl.ds(0, 4)], local_sem.at[1])
     landed(w, local_sem.at[2])
+    ids_arrive(2)
+    z_arrive(2, 0, 1)
+    for path in (0, 1):
+        p2_arrive(path, 1)
+    for path in (0, 1):
+        project_near(path, 0)
+    ids_arrive(3)
+    z_arrive(3, 0, 0)
+    for path in (0, 1):
+        p2_arrive(path, 2)
+    for path in (0, 1):
+        project_near(path, 1)
+    ids_arrive(4)
+    z_arrive(3, 0, 1)
+    for path in (0, 1):
+        p2_arrive(path, 3)
+    for path in (0, 1):
+        project_near(path, 2)
     make_tables()
-    z_arrive(1, 1)
-    project(0)
-    core_arrived(0, 0)
+    z_arrive(1, 1, 0)
+    select(0, 0)
+    z_arrive(1, 1, 1)
+    for path in (0, 1):
+        project_near(path, 3)
+    p2_far()
+    project_far()
     stats(0, 0)
-    z_arrive(4, 0)
-    z_arrive(2, 1)
-    core_arrived(0, 1)
+    z_arrive(4, 0, 0)
+    z_arrive(4, 0, 1)
+    z_arrive(2, 1, 0)
+    select(0, 1)
     stats(0, 1)
-    core_arrived(0, 2)
+    select(0, 2)
     stats(0, 2)
     stats_send(0)
-    project(1)
-    z_arrive(3, 1)
+    z_arrive(2, 1, 1)
+    z_arrive(3, 1, 0)
+    select(1, 0)
     stats_forward(0)
-    core_arrived(1, 0)
+    z_arrive(3, 1, 1)
     stats(1, 0)
     stats_arrived(0)
-    grads(0)
-    z_arrive(4, 1)
-    core_arrived(1, 1)
+    grads_begin(0)
+    grads_part(0, 0, 4, True)
+    z_arrive(4, 1, 0)
+    z_arrive(4, 1, 1)
+    grads_part(0, 4, 7, False)
+    grads_end(0)
+    weight_sibling(0, 0, 3)
+    select(1, 1)
     stats(1, 1)
-    core_arrived(1, 2)
+    select(1, 2)
     stats(1, 2)
     stats_send(1)
-    dq_send(0, 1, DP)
-    weight_sibling(0, 0, 3)
     weight_step(0, 1)
+    dq_send(0, (5, 6))
+    weight_sibling(0, 3, 8)
     stats_forward(1)
-    weight_sibling(0, 3, 8)
+    dq_send(0, (7, 0))
     weight_step(0, 2)
     stats_arrived(1)
-    grads(1)
+    grads_begin(1)
+    grads_part(1, 0, 7, False)
+    grads_end(1)
+    for path in (0, 1):
+        width_far(path)
     weight_sibling(1, 0, 3)
+    weight_step(0, 3)
     weight_step(1, 1)
-    dq_send(1, 1, DP)
-    weight_step(0, 3)
-    for path in (0, 1):
-        width_far(path)
+    dq_send(1, (1, 5))
+    for path in (0, 1):
+        width_near(path)
+    weight_step(0, 4)
     weight_sibling(1, 3, 8)
     weight_step(1, 2)
-    weight_step(0, 4)
-    for path in (0, 1):
-        width_near(path, 0)
+    dq_send(1, (2, 6))
+    for path in (0, 1):
+        width_own(path)
+    for way in (0, 1):
+        for path in (0, 1):
+            width_met(path, way)
     weight_step(1, 3)
-    for path in (0, 1):
-        width_near(path, 1)
+    dq_send(1, (3, 7))
     weight_final(0)
-    for path in (0, 1):
-        width_own(path)
+    dq_final(0)
     weight_step(1, 4)
-    dq_final(0)
+    dq_send(1, (4, 0))
+    for path in (0, 1):
+        width_turn(path)
     for path in (0, 1):
         width_second(path)
     for path in (0, 1):
         width_final(path)
+    weight_final(1)
     dq_final(1)
-    weight_final(1)
     finish()
 
 
@@ -670,6 +753,7 @@
             pltpu.VMEM((4, DP, 128), I32),
             pltpu.VMEM((MP, ROWS, SHARD), BF16),
             pltpu.VMEM((HEADS, MP * SHARD, 2 * HD), BF16),
+            pltpu.VMEM((HEADS, ROWS, 2 * HD), F32),
             pltpu.VMEM((ROWS, 2 * HD), F32),
             pltpu.VMEM((HEADS, ROWS, 2 * HD), BF16),
             pltpu.VMEM((HEADS, HD, ROWS), BF16),
@@ -688,13 +772,14 @@
             pltpu.VMEM((HEADS, 2, 4, SHARD, 2 * HD), BF16),
             pltpu.VMEM((2, 2, SIDE, CHUNK, SHARD), BF16),
             pltpu.VMEM((2, 2, SIDE, CHUNK, SHARD), BF16),
-            pltpu.VMEM((2, 2, SIDE, HALF, SHARD), BF16),
-            pltpu.VMEM((2, 2, SIDE, HALF, SHARD), BF16),
+            pltpu.VMEM((2, 2, SIDE, CHUNK, SHARD), F32),
+            pltpu.VMEM((2, 2, 2, SIDE, CHUNK, SHARD), BF16),
+            pltpu.VMEM((2, 2, 2, SIDE, CHUNK, SHARD), BF16),
             pltpu.VMEM((2, SIDE, HALF, SHARD), F32),
             pltpu.VMEM((2, 2, CHUNK, SHARD), BF16),
             pltpu.VMEM((2, 2, CHUNK, SHARD), BF16),
-            pltpu.VMEM((2, 2, HALF, SHARD), BF16),
-            pltpu.VMEM((2, 2, HALF, SHARD), BF16),
+            pltpu.VMEM((2, 2, 2, CHUNK, SHARD), BF16),
+            pltpu.VMEM((2, 2, 2, CHUNK, SHARD), BF16),
             dma((3,)), dma((22,)),
             dma((HEADS, 2, 2, 4)), dma((HEADS, 3)),
             dma((2, 4)), dma((1,)),

time: 145 us -> 123 us (0.85)
  Pallas kernels: 142 us -> 120 us
    pallas_call x1, Pallas kernels: 140 us -> 118 us  [body(): pl.pallas_call(kernel, out_shape=shapes, in_specs=[vmem] + [hbm] * 5, out...]
where the time goes in v3:
time: 123 us; the launch traced here: 122 us
  Pallas kernels  120 us (98%)
  local copies, waits for them, and re-layouts  1.44 us (1%)
    pallas_call x1, Pallas kernels, body(): pl.pallas_call(kernel, out_shape=shapes, in_specs=[vmem] + [hbm] * 5, out...  118 us

profile of v3, /device:TPU:2, one launch (start us, length us, event | category | flops | bytes accessed | tf_op | source)
XLA Modules:
  0.0 122.4 jit_solution(17902791565330230236)
XLA Ops:
  0.6 0.8 copy.11
  1.4 0.1 reshape.11
  1.5 0.6 pad.4.ids_ref
  2.1 118.2 %retro_backward.1 = (bf16[512,256]{1,0:T(8,128)(2,1)}, bf16[512,256]{1,0:T(8,128)(2,1)}, f32[256,256]{1,0:T(8,128)}, f32[256,256]{1,0:T(8,128)}) custom-call(s32[8,128]{1,0:T(8,128)} %pad.4.ids_ref, bf16[512,256]{1,0:T(8,128)(2,1)} %q_ref.1, bf16[512,256]{1,0:T(8,128)(2,1)} %g_ref.1, bf16[512,256]{1,0:T(8,128)(2,1)} %e_ref.1, bf16[4096,256]{1,0:T(8,128)(2,1)} %kw_ref.1, ...), custom_call_target="tpu_custom_call" | custom-call | tf_op jit(solution)/shard_map/retro_backward/pallas_call | solution.py:744
  120.2 2.2 %publish.1 = (bf16[512,256]{1,0:T(8,128)(2,1)}, bf16[512,256]{1,0:T(8,128)(2,1)}, f32[256,256]{1,0:T(8,128)}, f32[256,256]{1,0:T(8,128)}) custom-call(bf16[512,256]{1,0:T(8,128)(2,1)} %get-tuple-element.8.a, bf16[512,256]{1,0:T(8,128)(2,1)} %get-tuple-element.9.b, f32[256,256]{1,0:T(8,128)} %get-tuple-element.10.c, f32[256,256]{1,0:T(8,128)} %get-tuple-element.11.d), custom_call_target="tpu_custom_call" | custom-call | tf_op jit(solution)/shard_map/publish/pallas_call | solution.py:796

commit v4 on v3

--- a/solution.py
+++ b/solution.py
@@ -66,7 +66,7 @@
 
     def greet(self):
         barrier = pltpu.get_barrier_semaphore()
-        others = [(wrap(self.dp + k, DP), self.mp) for k in range(1, DP)]
+        others = [self.z_device(0), self.z_device(1), (self.sibling, self.mp)]
         others += [(self.dp, self.plane_neighbour(0, axis, way)) for axis in (0, 1) for way in (0, 1)]
         for device in others:
             pl.semaphore_signal(barrier, inc=1, device_id=device, device_id_type=MESH)
@@ -691,20 +691,21 @@
     grads_begin(1)
     grads_part(1, 0, 7, False)
     grads_end(1)
-    for path in (0, 1):
-        width_far(path)
     weight_sibling(1, 0, 3)
+    width_far(0)
+    width_far(1)
     weight_step(0, 3)
     weight_step(1, 1)
+    dq_send(1, (4, 0))
+    width_near(0)
+    width_near(1)
+    weight_step(0, 4)
     dq_send(1, (1, 5))
-    for path in (0, 1):
-        width_near(path)
-    weight_step(0, 4)
     weight_sibling(1, 3, 8)
     weight_step(1, 2)
     dq_send(1, (2, 6))
-    for path in (0, 1):
-        width_own(path)
+    width_own(0)
+    width_own(1)
     for way in (0, 1):
         for path in (0, 1):
             width_met(path, way)
@@ -712,16 +713,15 @@
     dq_send(1, (3, 7))
     weight_final(0)
     dq_final(0)
+    for path in (0, 1):
+        width_turn(path)
     weight_step(1, 4)
-    dq_send(1, (4, 0))
-    for path in (0, 1):
-        width_turn(path)
     for path in (0, 1):
         width_second(path)
+    dq_final(1)
     for path in (0, 1):
         width_final(path)
     weight_final(1)
-    dq_final(1)
     finish()
 
 

time: 123 us -> 119 us (0.967)
  Pallas kernels: 120 us -> 116 us
    pallas_call x1, Pallas kernels: 118 us -> 114 us  [body(): pl.pallas_call(kernel, out_shape=shapes, in_specs=[vmem] + [hbm] * 5, out...]
where the time goes in v4:
time: 119 us; the launch traced here: 118 us
  Pallas kernels  116 us (97%)
  local copies, waits for them, and re-layouts  1.44 us (1%)
    pallas_call x1, Pallas kernels, body(): pl.pallas_call(kernel, out_shape=shapes, in_specs=[vmem] + [hbm] * 5, out...  114 us

profile of v4, /device:TPU:2, one launch (start us, length us, event | category | flops | bytes accessed | tf_op | source)
XLA Modules:
  0.0 118.1 jit_solution(15570917088597390022)
XLA Ops:
  0.6 0.8 copy.11
  1.4 0.1 reshape.11
  1.5 0.6 pad.4.ids_ref
  2.1 113.9 %retro_backward.1 = (bf16[512,256]{1,0:T(8,128)(2,1)}, bf16[512,256]{1,0:T(8,128)(2,1)}, f32[256,256]{1,0:T(8,128)}, f32[256,256]{1,0:T(8,128)}) custom-call(s32[8,128]{1,0:T(8,128)} %pad.4.ids_ref, bf16[512,256]{1,0:T(8,128)(2,1)} %q_ref.1, bf16[512,256]{1,0:T(8,128)(2,1)} %g_ref.1, bf16[512,256]{1,0:T(8,128)(2,1)} %e_ref.1, bf16[4096,256]{1,0:T(8,128)(2,1)} %kw_ref.1, ...), custom_call_target="tpu_custom_call" | custom-call | tf_op jit(solution)/shard_map/retro_backward/pallas_call | solution.py:744
  115.9 2.2 %publish.1 = (bf16[512,256]{1,0:T(8,128)(2,1)}, bf16[512,256]{1,0:T(8,128)(2,1)}, f32[256,256]{1,0:T(8,128)}, f32[256,256]{1,0:T(8,128)}) custom-call(bf16[512,256]{1,0:T(8,128)(2,1)} %get-tuple-element.8.a, bf16[512,256]{1,0:T(8,128)(2,1)} %get-tuple-element.9.b, f32[256,256]{1,0:T(8,128)} %get-tuple-element.10.c, f32[256,256]{1,0:T(8,128)} %get-tuple-element.11.d), custom_call_target="tpu_custom_call" | custom-call | tf_op jit(solution)/shard_map/publish/pallas_call | solution.py:796

commit v5 on v4

--- a/solution.py
+++ b/solution.py
@@ -725,9 +725,17 @@
     finish()
 
 
-def publish_kernel(a, b, c, d, a_out, b_out, c_out, d_out):
-    for src, dst in ((a, a_out), (b, b_out), (c, c_out), (d, d_out)):
-        dst[...] = src[...]
+def publish_kernel(a, b, c, d, a_out, b_out, c_out, d_out, a_mid, b_mid, c_mid, d_mid, came, left):
+    arrays = ((a, a_mid, a_out), (b, b_mid, b_out), (c, c_mid, c_out), (d, d_mid, d_out))
+    loads = [pltpu.make_async_copy(x[0], x[1], came.at[n]) for n, x in enumerate(arrays)]
+    stores = [pltpu.make_async_copy(x[1], x[2], left.at[n]) for n, x in enumerate(arrays)]
+    for load in loads:
+        load.start()
+    for load, store in zip(loads, stores):
+        load.wait()
+        store.start()
+    for store in stores:
+        store.wait()
 
 
 def body(queries, grad_attn, encoded, key_weight, value_weight, nbr_ids):
@@ -796,8 +804,9 @@
     return pl.pallas_call(
         publish_kernel,
         out_shape=shapes,
-        in_specs=[vmem] * 4,
-        out_specs=(vmem,) * 4,
+        in_specs=[hbm] * 4,
+        out_specs=(hbm,) * 4,
+        scratch_shapes=[pltpu.VMEM(x.shape, x.dtype) for x in shapes] + [dma((4,)), dma((4,))],
         name="publish",
     )(*results)
 

time: 119 us -> 119 us (level)
  no operation moved by 1% of the time
where the time goes in v5:
time: 119 us; the launch traced here: 118 us
  Pallas kernels  116 us (97%)
  local copies, waits for them, and re-layouts  1.44 us (1%)
    pallas_call x1, Pallas kernels, body(): pl.pallas_call(kernel, out_shape=shapes, in_specs=[vmem] + [hbm] * 5, out...  114 us

profile of v5, /device:TPU:2, one launch (start us, length us, event | category | flops | bytes accessed | tf_op | source)
XLA Modules:
  0.0 117.9 jit_solution(13239991596136129515)
XLA Ops:
  0.6 0.8 copy.11
  1.4 0.1 reshape.11
  1.5 0.6 pad.4.ids_ref
  2.1 113.9 %retro_backward.1 = (bf16[512,256]{1,0:T(8,128)(2,1)}, bf16[512,256]{1,0:T(8,128)(2,1)}, f32[256,256]{1,0:T(8,128)}, f32[256,256]{1,0:T(8,128)}) custom-call(s32[8,128]{1,0:T(8,128)} %pad.4.ids_ref, bf16[512,256]{1,0:T(8,128)(2,1)} %q_ref.1, bf16[512,256]{1,0:T(8,128)(2,1)} %g_ref.1, bf16[512,256]{1,0:T(8,128)(2,1)} %e_ref.1, bf16[4096,256]{1,0:T(8,128)(2,1)} %kw_ref.1, ...), custom_call_target="tpu_custom_call" | custom-call | tf_op jit(solution)/shard_map/retro_backward/pallas_call | solution.py:752
  115.9 2.0 %publish.1 = (bf16[512,256]{1,0:T(8,128)(2,1)}, bf16[512,256]{1,0:T(8,128)(2,1)}, f32[256,256]{1,0:T(8,128)}, f32[256,256]{1,0:T(8,128)}) custom-call(bf16[512,256]{1,0:T(8,128)(2,1)} %get-tuple-element.8.a, bf16[512,256]{1,0:T(8,128)(2,1)} %get-tuple-element.9.b, f32[256,256]{1,0:T(8,128)} %get-tuple-element.10.c, f32[256,256]{1,0:T(8,128)} %get-tuple-element.11.d), custom_call_target="tpu_custom_call" | custom-call | tf_op jit(solution)/shard_map/publish/pallas_call | solution.py:804
